TPU v7x, 32 devices: a whole 2x2x4 slice. The times are simulated.
32 devices in a mesh: groups: 2 (over x), tensor: 16 (over z, y, core).
Axes of the slice: x: 2, y: 2, z: 4, core: 2. Of those that a mesh axis runs over, the one named last changes fastest.
Arguments:
- hidden: bfloat16 [256, 16384], P(('groups', 'tensor')), parts along dimension 0, as said below
- positions: int32 [256], P('groups'), parts along dimension 0, may hold values from 0 to 63, as said below
- norm_in: float32 [16384], replicated, may hold values from 0.1 to 1.9
- w_query: bfloat16 [16384, 2048], P(None, 'tensor'), as said below
- w_key: bfloat16 [16384, 1024], P(None, 'tensor'), as said below
- w_value: bfloat16 [16384, 1024], P(None, 'tensor'), may hold values from -0.046875 to 0.046875
- w_out: bfloat16 [2048, 16384], P('tensor'), may hold values from -0.125 to 0.125
- norm_out: float32 [16384], replicated, may hold values from 0.1 to 1.9
- w_next: bfloat16 [16384, 2048], P(None, 'tensor'), may hold values from -0.046875 to 0.046875
Outputs:
- residual_out: bfloat16 [256, 16384], P(('groups', 'tensor')), parts along dimension 0
- query_next: bfloat16 [256, 2048], P('groups', 'tensor'), parts along dimension 0
There are 2 independent parts, one for each index of `groups`. A program takes and returns all parts, laid end to end along the dimension named above; an argument that names none is the same for every part. Nothing has to cross between parts.
Inputs may be any that keep to these rules, and one draw needn't show every extreme that they name: Within each packed document positions rise by one from 0; a document begins where the position is 0, and token 0 begins one. `w_key`: A dense random matrix of fan-in 16384. `w_query`: A dense random matrix of fan-in 16384. `hidden`: rows and features carry scales of their own.
All inputs are finite; a program needn't handle non-finite values.
Results may differ from a plain program's by a relative error of at most 0.0062.
Values may be sent and summed in bfloat16 or wider, within the bound.
A program may use at most 128 MiB of HBM per device.

v0:
```python
import math

import jax
import jax.numpy as jnp
from jax import lax
from jax.sharding import PartitionSpec as P

KVH = 8
HB = 128


def normalize(values, gain):
    mean_square = jnp.mean(values * values, axis=-1, keepdims=True)
    return values * lax.rsqrt(mean_square + 1e-05) * gain


def rotary(values, positions, head_dim):
    count = values.shape[0]
    heads_here = values.shape[1] // head_dim
    half = head_dim // 2
    shaped = values.reshape(count, heads_here, head_dim)
    inverse = jnp.exp(-math.log(500000.0) * (2.0 * jnp.arange(half, dtype=jnp.float32) / head_dim))
    angle = positions.astype(jnp.float32)[:, None] * inverse[None, :]
    cosine = jnp.cos(angle)[:, None, :]
    sine = jnp.sin(angle)[:, None, :]
    first = shaped[:, :, :half]
    second = shaped[:, :, half:]
    turned = jnp.concatenate(
        [first * cosine - second * sine, second * cosine + first * sine], axis=-1
    )
    return turned.reshape(count, heads_here * head_dim)


def attend(query, key_block, value_block, positions):
    count = positions.shape[0]
    order = jnp.arange(count, dtype=jnp.int32)
    allowed = (order[:, None] >= order[None, :]) & (
        positions[:, None] - positions[None, :] == order[:, None] - order[None, :]
    )
    scores = jnp.dot(query, key_block.T, preferred_element_type=jnp.float32) * (
        1.0 / math.sqrt(query.shape[1])
    )
    scores = jnp.where(allowed, scores, -1e30)
    largest = jnp.max(scores, axis=-1, keepdims=True)
    weights = jnp.where(allowed, jnp.exp(scores - largest), 0.0)
    weights = (weights / jnp.sum(weights, axis=-1, keepdims=True)).astype(jnp.bfloat16)
    return jnp.dot(weights, value_block, preferred_element_type=jnp.float32).astype(jnp.bfloat16)


def hadamard_table(block):
    row_index = jnp.arange(block, dtype=jnp.int32)[:, None]
    column_index = jnp.arange(block, dtype=jnp.int32)[None, :]
    parity = jnp.zeros((block, block), jnp.int32)
    for level in range(block.bit_length() - 1):
        parity = parity + (jnp.right_shift(row_index, level) & 1) * (
            jnp.right_shift(column_index, level) & 1
        )
    return (1 - 2 * (parity % 2)).astype(jnp.float32) * (1.0 / math.sqrt(block))


def on_device(hidden, positions, norm_in, w_query, w_key, w_value, w_out, norm_out, w_next):
    width = lax.axis_size("tensor")
    rank = lax.axis_index("tensor")
    tokens = positions.shape[0]
    share = hidden.shape[0]
    features = hidden.shape[1]
    head_dim = w_query.shape[1]
    key_cols = w_key.shape[1]
    blocks = features // HB
    table = hadamard_table(HB)

    def rotate(values):
        shaped = values.reshape(values.shape[:-1] + (blocks, HB))
        turned = jnp.einsum("...bk,kl->...bl", shaped, table, precision=lax.Precision.HIGHEST)
        return turned.reshape(values.shape)

    residual = hidden.astype(jnp.float32)
    x_in = normalize(residual, norm_in).astype(jnp.bfloat16)
    w_input = jnp.concatenate([w_query, w_key, w_value], axis=1)
    projected = jnp.dot(
        lax.all_gather(x_in, "tensor", axis=0, tiled=True),
        w_input,
        preferred_element_type=jnp.float32,
    )
    queries = rotary(projected[:, :head_dim], positions, head_dim).astype(jnp.bfloat16)
    key_raw = projected[:, head_dim : head_dim + key_cols].astype(jnp.bfloat16)
    value_local = projected[:, head_dim + key_cols :].astype(jnp.bfloat16)
    key_all, value_all = (
        lax.all_gather(key_raw, "tensor", axis=1, tiled=True),
        lax.all_gather(value_local, "tensor", axis=1, tiled=True),
    )
    group = rank // (width // KVH)
    key_block = lax.dynamic_index_in_dim(
        key_all.reshape(tokens, head_dim, KVH), group, 2, keepdims=False
    )
    key_block = rotary(key_block.astype(jnp.float32), positions, head_dim).astype(jnp.bfloat16)
    value_block = lax.dynamic_index_in_dim(
        value_all.reshape(tokens, head_dim, KVH), group, 2, keepdims=False
    )
    context = attend(queries, key_block, value_block, positions)
    rotated = rotate(jnp.dot(context, w_out, preferred_element_type=jnp.float32))
    shaped = rotated.reshape(tokens, blocks, HB)
    peak = jnp.max(jnp.abs(shaped), axis=-1)
    scale = jnp.exp2(jnp.ceil(jnp.log2(peak / 127.0 + 1e-30)))
    packed = (shaped / scale[:, :, None]).astype(jnp.bfloat16).reshape(tokens, features)
    received, received_scale = (
        lax.all_to_all(packed, "tensor", split_axis=0, concat_axis=0, tiled=True),
        lax.all_to_all(
            scale.astype(jnp.bfloat16), "tensor", split_axis=0, concat_axis=0, tiled=True
        ).astype(scale.dtype),
    )
    terms = received.reshape(width, share, blocks, HB).astype(jnp.float32) * received_scale.reshape(
        width, share, blocks, 1
    )
    mixed = jnp.sum(terms, axis=0).reshape(share, features)
    residual_f = residual + rotate(mixed)
    residual_out = residual_f.astype(jnp.bfloat16)
    x_next = normalize(residual_f, norm_out).astype(jnp.bfloat16)
    next_raw = jnp.dot(
        lax.all_gather(x_next, "tensor", axis=0, tiled=True),
        w_next,
        preferred_element_type=jnp.float32,
    )
    query_next = rotary(next_raw, positions, head_dim).astype(jnp.bfloat16)
    return (residual_out, query_next)


def solution(mesh):
    placed = (
        P(("groups", "tensor"), None),
        P("groups"),
        P(),
        P(None, "tensor"),
        P(None, "tensor"),
        P(None, "tensor"),
        P("tensor", None),
        P(),
        P(None, "tensor"),
    )
    return jax.shard_map(
        on_device,
        mesh=mesh,
        in_specs=placed,
        out_specs=(P(("groups", "tensor"), None), P("groups", "tensor")),
        check_vma=False,
    )
```

profile of v0, /device:TPU:0, one launch (start us, length us, event | category | flops | bytes accessed | tf_op | source)
XLA Modules:
  0.0 326.7 jit_solution(14954889090827007191)
XLA Ops:
  7.2 1.3 fusion.8
  8.6 1.8 fusion.10
  10.4 0.7 convert_element_type.75
  11.1 4.9 %copy.27 = bf16[16384,64]{1,0:T(8,128)(2,1)} copy(bf16[16384,64]{0,1:T(8,128)(2,1)} %param.13) | data formatting | bytes 4194304 | tf_op args[4]
  15.9 3.2 copy.28
  19.2 44.9 %all-gather.3.cloned.1.call-done = bf16[128,16384]{1,0:T(8,128)(2,1)} async-done(((bf16[8,16384]{1,0:T(8,128)(2,1)}), bf16[128,16384]{1,0:T(8,128)(2,1)}) %all-gather.3.cloned.1.call-update) | async-done | bytes 4194320 | tf_op jit(solution)/shard_map/all_gather | solution.py:81
  64.0 8.3 %fusion.110 = (bf16[128,256]{1,0:T(8,128)(2,1)S(1)}, f32[128,256]{1,0:T(8,128)S(1)}) fusion(bf16[128,16384]{1,0:T(8,128)(2,1)} %all-gather.3.cloned.1.call-done, bf16[16384,64]{1,0:T(8,128)(2,1)} %copy.28, bf16[16384,64]{1,0:T(8,128)(2,1)} %copy.27, bf16[16384,128]{1,0:T(8,128)(2,1)} %param.12), kind=kOutput, calls=%fused_computation.140 | convolution fusion | flops 1098940416 | bytes 12779520 | tf_op jit(solution)/shard_map/dot_general | solution.py:80
  72.7 19.6 %all_gather.13 = bf16[128,1024]{0,1:T(8,128)(2,1)S(1)} all-gather(bf16[128,64]{0,1:T(8,128)(2,1)S(1)} %copy.29), channel_id=1, replica_groups=mesh['groups'=2,'tensor'=16] {'tensor'}, dimensions={1}, use_global_device_ids=true | all-gather | bytes 278528 | tf_op jit(solution)/shard_map/all_gather | solution.py:89
  92.3 18.1 %all_gather.14 = bf16[128,1024]{0,1:T(8,128)(2,1)S(1)} all-gather(bf16[128,64]{0,1:T(8,128)(2,1)S(1)} %copy.31), channel_id=1, replica_groups=mesh['groups'=2,'tensor'=16] {'tensor'}, dimensions={1}, use_global_device_ids=true | all-gather | bytes 278528 | tf_op jit(solution)/shard_map/all_gather | solution.py:90
  110.4 0.1 constant_dynamic-slice_fusion
  110.7 0.1 copy.40
  110.8 0.3 fusion.94
  111.2 0.3 fusion.111
  111.6 6.9 %convolution_bitcast_fusion = f32[16,8,128,128]{3,1,2,0:T(8,128)} fusion(bf16[128,16384]{1,0:T(8,128)(2,1)} %param.15, f32[128,128]{0,1:T(8,128)S(1)} %get-tuple-element.19, bf16[128,128,1]{1,0,2:T(8,128)(2,1)S(1)} %copy.32, f32[128]{0:T(128)S(1)} %fusion.45, f32[128]{0:T(128)S(1)} %get-tuple-element.18, s32[128]{0:T(128)S(1)} %copy-done.3), kind=kOutput, calls=%fused_computation.10 | convolution fusion | flops 541229056 | bytes 12682752 | tf_op jit(solution)/shard_map/dot_general | solution.py:101
  118.5 4.8 %copy.41 = f32[16,8,128,128]{3,2,1,0:T(8,128)S(1)} copy(f32[16,8,128,128]{3,1,2,0:T(8,128)} %convolution_bitcast_fusion) | data formatting | bytes 16777216
  123.3 9.9 %abs_reduce_fusion = (f32[128,128]{1,0:T(8,128)S(1)}, f32[128,128,128]{1,2,0:T(8,128)}) fusion(f32[128,128,128]{2,1,0:T(8,128)S(1)} %bitcast.58, s32[128]{0:T(128)S(1)} %get-tuple-element.24, s32[128]{0:T(128)S(1)} %get-tuple-element.25, s32[128]{0:T(128)S(1)} %get-tuple-element.26, s32[128]{0:T(128)S(1)} %get-tuple-element.27, ...), kind=kOutput, calls=%fused_computation.9 | convolution fusion | flops 3225862144 | bytes 16846336 | tf_op jit(solution)/shard_map/...bk,kl->...bl/dot_general | solution.py:74
  133.2 0.6 convert_bitcast_fusion
  133.9 3.7 %all-to-all-start.1 = ((bf16[16,8,128]{2,1,0:T(8,128)(2,1)}), bf16[16,8,128]{2,1,0:T(8,128)(2,1)S(1)}, u32[]{:S(2)}, u32[]{:S(2)}) async-start(bf16[16,8,128]{2,1,0:T(8,128)(2,1)} %get-tuple-element.10), calls=%async_computation.1 | async-start | bytes 65536 | tf_op jit(solution)/shard_map/all_to_all | solution.py:108
  137.6 6.7 %divide_convert_fusion = bf16[128,128,128]{1,2,0:T(8,128)(2,1)} fusion(f32[128,128,128]{1,2,0:T(8,128)} %get-tuple-element.21, f32[128,128]{1,0:T(8,128)S(1)} %get-tuple-element.11), kind=kLoop, calls=%fused_computation.8 | loop fusion | flops 4194304 | bytes 12648448 | tf_op jit(solution)/shard_map/convert_element_type | solution.py:105
  144.3 6.4 %copy.33 = bf16[128,128,128]{2,1,0:T(8,128)(2,1)} copy(bf16[128,128,128]{1,2,0:T(8,128)(2,1)} %divide_convert_fusion) | data formatting | bytes 8388608 | tf_op jit(solution)/shard_map/convert_element_type | solution.py:105
  150.7 7.4 %all_to_all.10 = bf16[16,8,16384]{2,1,0:T(8,128)(2,1)} reshape(bf16[128,128,128]{2,1,0:T(8,128)(2,1)} %copy.33) | data formatting | bytes 8388608 | tf_op jit(solution)/shard_map/all_to_all | solution.py:107
  158.1 6.0 %all-to-all-start = ((bf16[16,8,16384]{2,1,0:T(8,128)(2,1)}), bf16[16,8,16384]{2,1,0:T(8,128)(2,1)}, u32[]{:S(2)}, u32[]{:S(2)}) async-start(bf16[16,8,16384]{2,1,0:T(8,128)(2,1)} %all_to_all.10), calls=%async_computation | async-start | bytes 8388608 | tf_op jit(solution)/shard_map/all_to_all | solution.py:107
  164.2 0.2 copy.34
  164.4 77.4 %all-to-all-done = bf16[16,8,16384]{2,1,0:T(8,128)(2,1)} async-done(((bf16[16,8,16384]{2,1,0:T(8,128)(2,1)}), bf16[16,8,16384]{2,1,0:T(8,128)(2,1)}, u32[]{:S(2)}, u32[]{:S(2)}) %all-to-all-start) | async-done | bytes 4194336 | tf_op jit(solution)/shard_map/all_to_all | solution.py:107
  241.8 4.4 %fusion.6 = f32[8,16384]{1,0:T(8,128)S(1)} fusion(bf16[16,8,16384]{2,1,0:T(8,128)(2,1)} %all-to-all-done, f32[16,8,128]{1,2,0:T(8,128)S(1)} %copy.34), kind=kLoop, calls=%fused_computation.7 | loop fusion | flops 6160384 | bytes 4784128 | tf_op jit(solution)/shard_map/reduce_sum | solution.py:115
  246.2 0.8 convolution_bitcast_fusion.1
  247.0 0.4 multiply_reduce_fusion
  247.4 1.1 multiply_convert_fusion
  248.5 65.6 %all-gather.5.cloned.1.call-done = bf16[128,16384]{1,0:T(8,128)(2,1)} async-done(((bf16[8,16384]{1,0:T(8,128)(2,1)}), bf16[128,16384]{1,0:T(8,128)(2,1)}) %all-gather.5.cloned.1.call-update) | async-done | bytes 4194320 | tf_op jit(solution)/shard_map/all_gather | solution.py:120
  314.1 4.7 %convolution_bitcast_fusion.2 = f32[128,1,128]{2,0,1:T(8,128)S(1)} fusion(bf16[128,16384]{1,0:T(8,128)(2,1)} %all-gather.5.cloned.1.call-done, bf16[16384,128]{1,0:T(8,128)(2,1)} %param.17), kind=kOutput, calls=%fused_computation.12 | convolution fusion | flops 536870912 | bytes 8454144 | tf_op jit(solution)/shard_map/dot_general | solution.py:119
  318.9 0.3 fusion.35
  319.2 0.7 maximum_bitcast_fusion
  (27 shorter events, 0.7 us)
Async XLA Ops:
  7.2 8.8 %copy-start.1 = (bf16[16384,64]{0,1:T(8,128)(2,1)S(1)}, bf16[16384,64]{0,1:T(8,128)(2,1)}, u32[]{:S(2)}) copy-start(bf16[16384,64]{0,1:T(8,128)(2,1)} %param.14) | copy-start | bytes 6291460
  7.2 56.9 %all-gather.3.cloned.1.call-start = ((), (), s32[]{:S(2)}) async-start(), calls=%async_computation.2 | async-start | bytes 4456448 | tf_op jit(solution)/shard_map/all_gather | solution.py:81
  19.1 92.0 %copy-start.3 = (s32[128]{0:T(128)S(1)}, s32[128]{0:T(128)}, u32[]{:S(2)}) copy-start(s32[128]{0:T(128)} %param.10) | copy-start | bytes 1540
  133.9 24.2 %all-to-all-start.1 = ((bf16[16,8,128]{2,1,0:T(8,128)(2,1)}), bf16[16,8,128]{2,1,0:T(8,128)(2,1)S(1)}, u32[]{:S(2)}, u32[]{:S(2)}) async-start(bf16[16,8,128]{2,1,0:T(8,128)(2,1)} %get-tuple-element.10), calls=%async_computation.1 | async-start | bytes 65536 | tf_op jit(solution)/shard_map/all_to_all | solution.py:108
  158.1 83.7 %all-to-all-start = ((bf16[16,8,16384]{2,1,0:T(8,128)(2,1)}), bf16[16,8,16384]{2,1,0:T(8,128)(2,1)}, u32[]{:S(2)}, u32[]{:S(2)}) async-start(bf16[16,8,16384]{2,1,0:T(8,128)(2,1)} %all_to_all.10), calls=%async_computation | async-start | bytes 8388608 | tf_op jit(solution)/shard_map/all_to_all | solution.py:107
  164.1 82.9 %copy-start = (bf16[8,16384]{1,0:T(8,128)(2,1)S(1)}, bf16[8,16384]{1,0:T(8,128)(2,1)}, u32[]{:S(2)}) copy-start(bf16[8,16384]{1,0:T(8,128)(2,1)} %param.9) | copy-start | bytes 786436
  164.1 83.3 %copy-start.2 = (f32[16384]{0:T(1024)S(1)}, f32[16384]{0:T(1024)}, u32[]{:S(2)}) copy-start(f32[16384]{0:T(1024)} %param.16) | copy-start | bytes 196612
  164.1 150.0 %all-gather.5.cloned.1.call-start = ((), (), s32[]{:S(2)}) async-start(), calls=%async_computation.3 | async-start | bytes 4456448 | tf_op jit(solution)/shard_map/all_gather | solution.py:120
Sparse Core Ops, SparseCore 0:
  10.7 53.2 all-gather.2
  248.6 65.4 all-gather.4
where the time goes:
time: 328 us; the launch traced here: 327 us
  waiting for transfers between devices  188 us (57%)
  blocking collectives  37.7 us (11%)
  matrix products  30.9 us (9%)
  local copies, waits for them, and re-layouts  27.5 us (8%)
  other arithmetic  18.6 us (6%)
  between operations  14.3 us (4%)
  starting transfers between devices  9.78 us (3%)
    all_to_all x1, waiting for transfers between devices, on_device(): lax.all_to_all(packed, 'tensor', split_axis=0, concat_axis=0, tiled=True)  77.4 us
    all_gather x1, waiting for transfers between devices, on_device(): lax.all_gather(x_next, 'tensor', axis=0, tiled=True)  65.6 us
    all_gather x1, waiting for transfers between devices, on_device(): lax.all_gather(x_in, 'tensor', axis=0, tiled=True)  44.9 us
    all_gather x1, blocking collectives, on_device(): lax.all_gather(key_raw, 'tensor', axis=1, tiled=True)  19.6 us
    all_gather x1, blocking collectives, on_device(): lax.all_gather(value_local, 'tensor', axis=1, tiled=True)  18.1 us
    unnamed x12, local copies, waits for them, and re-layouts  13 us
    dot_general x2, matrix products, rotate(): jnp.einsum('...bk,kl->...bl', shaped, table, precision=lax.Precision.HIGH...  10.7 us
    dot_general x1, matrix products, on_device(): jnp.dot(lax.all_gather(x_in, 'tensor', axis=0, tiled=True), w_input, pref...  8.34 us
  transfers between devices with their start and end apart: 4, of which 3 were waited for; matrix products, arithmetic and copies ran while one was open for 7% of the time, Pallas kernels for 0%

commit v1 on v0

v1 whole, which is shorter than its diff:
```python
import math

import jax
import jax.numpy as jnp
from jax import lax
from jax.experimental import pallas as pl
from jax.experimental.pallas import tpu as pltpu
from jax.sharding import PartitionSpec as P

KVH = 8
CHUNKS = 4
F32 = jnp.float32
BF16 = jnp.bfloat16


def normalize(values, gain):
    mean_square = jnp.mean(values * values, axis=-1, keepdims=True)
    return values * lax.rsqrt(mean_square + 1e-05) * gain


def rotary(values, positions, head_dim):
    count = values.shape[0]
    heads_here = values.shape[1] // head_dim
    half = head_dim // 2
    shaped = values.reshape(count, heads_here, head_dim)
    inverse = jnp.exp(-math.log(500000.0) * (2.0 * jnp.arange(half, dtype=jnp.float32) / head_dim))
    angle = positions.astype(jnp.float32)[:, None] * inverse[None, :]
    cosine = jnp.cos(angle)[:, None, :]
    sine = jnp.sin(angle)[:, None, :]
    first = shaped[:, :, :half]
    second = shaped[:, :, half:]
    turned = jnp.concatenate(
        [first * cosine - second * sine, second * cosine + first * sine], axis=-1
    )
    return turned.reshape(count, heads_here * head_dim)


def attend(query, key_block, value_block, positions):
    count = positions.shape[0]
    order = jnp.arange(count, dtype=jnp.int32)
    allowed = (order[:, None] >= order[None, :]) & (
        positions[:, None] - positions[None, :] == order[:, None] - order[None, :]
    )
    scores = jnp.dot(query, key_block.T, preferred_element_type=jnp.float32) * (
        1.0 / math.sqrt(query.shape[1])
    )
    scores = jnp.where(allowed, scores, -1e30)
    largest = jnp.max(scores, axis=-1, keepdims=True)
    weights = jnp.where(allowed, jnp.exp(scores - largest), 0.0)
    weights = (weights / jnp.sum(weights, axis=-1, keepdims=True)).astype(jnp.bfloat16)
    return jnp.dot(weights, value_block, preferred_element_type=jnp.float32).astype(jnp.bfloat16)


def block_kernel(
    hid, pos, gain_in, gain_out, wq_hbm, wk_hbm, wv_hbm, wo_hbm, wn_hbm,
    res_out, next_out,
    wq, wk, wv, wo, wn, xg1, xg2, part, rb1, s1, rb2, s2, up_out, up_in, down_out, down_in,
    kvs, kvr, acc, acc_next, squares, ctx,
    w_sem, ag_send, ag_recv, kv_send, kv_recv, sib_send, sib_recv, y_send, y_recv,
    up_send, up_recv, down_send, down_recv,
):
    me = lax.axis_index("tensor")
    c, y, z = lax.rem(me, 2), lax.rem(me // 2, 2), me // 4
    width = 16
    features = hid.shape[1]
    half = features // 2
    cw = half // CHUNKS
    tile = min(512, cw)
    tiles = cw // tile

    def index(zz, yy, cc):
        return (zz * 2 + yy) * 2 + cc

    sibling, across = index(z, y, 1 - c), index(z, 1 - y, c)
    upper, lower = index(z + 1, y, c), index(z - 1, y, c)
    pending = []

    def remote(src, dst, send, recv, device):
        return pltpu.make_async_remote_copy(
            src_ref=src, dst_ref=dst, send_sem=send, recv_sem=recv,
            device_id={"tensor": device}, device_id_type=pl.DeviceIdType.MESH,
        )

    def launch(make, when=None):
        if when is None:
            make().start()
        else:
            pl.when(when)(lambda: make().start())
        pending.append((make, when))

    weights = [
        pltpu.make_async_copy(src, dst, w_sem.at[i])
        for i, (src, dst) in enumerate(
            [(wq_hbm, wq), (wk_hbm, wk), (wv_hbm, wv), (wo_hbm, wo), (wn_hbm, wn)]
        )
    ]
    for copy in weights:
        copy.start()

    barrier = pltpu.get_barrier_semaphore()
    for step in range(1, width):
        pl.semaphore_signal(
            barrier, inc=1, device_id={"tensor": lax.rem(me + step, width)},
            device_id_type=pl.DeviceIdType.MESH,
        )

    def hidden_rows(k, off, size):
        first = hid[:, pl.ds(k * cw + off, size)].astype(F32)
        second = hid[:, pl.ds(half + k * cw + off, size)].astype(F32)
        return jnp.concatenate([first, second], axis=0)

    for k in range(CHUNKS):
        xg1[k, me] = hidden_rows(k, 0, cw).astype(BF16)
    acc[...] = jnp.zeros_like(acc)
    acc_next[...] = jnp.zeros_like(acc_next)
    squares[...] = jnp.zeros_like(squares)
    pl.semaphore_wait(barrier, width - 1)

    def gather_stages(a, xg):
        def copy(k, origin, slot, device):
            return lambda: remote(
                xg.at[k, origin], xg.at[k, origin], ag_send.at[a, k, slot], ag_recv.at[a, k, origin], device
            )

        def arrived(k, origin):
            copy(k, origin, 0, sibling)().wait_recv()

        def own(k):
            launch(copy(k, me, 0, upper), z < 3)
            launch(copy(k, me, 1, lower), z > 0)
            launch(copy(k, me, 2, across))
            launch(copy(k, me, 3, sibling))

        sides = [(d, s) for d in (1, 2, 3) for s in (0, 1)]

        def where(d, s):
            return (z - d, z >= d) if s == 0 else (z + d, z + d <= 3)

        def along(d):
            def stage(k):
                for s in (0, 1):
                    zz, there = where(d, s)
                    origin = index(zz, y, c)
                    slot = 4 + 3 * sides.index((d, s))
                    pl.when(there)(lambda: arrived(k, origin))
                    launch(copy(k, origin, slot, across), there)
                    if d < 3:
                        if s == 0:
                            launch(copy(k, origin, slot + 1, upper), there & (z < 3))
                        else:
                            launch(copy(k, origin, slot + 1, lower), there & (z > 0))
                    launch(copy(k, origin, slot + 2, sibling), there)
            return stage

        def over(d):
            def stage(k):
                if d == 0:
                    origin = index(z, 1 - y, c)
                    arrived(k, origin)
                    launch(copy(k, origin, 22, sibling))
                    return
                for s in (0, 1):
                    zz, there = where(d, s)
                    origin = index(zz, 1 - y, c)
                    pl.when(there)(lambda: arrived(k, origin))
                    launch(copy(k, origin, 23 + sides.index((d, s)), sibling), there)
            return stage

        def last(k):
            for j in range(8):
                arrived(k, j * 2 + 1 - c)

        return own, along, over, last

    def run(stages):
        for step in range(CHUNKS + max(delay for delay, _ in stages)):
            for delay, stage in stages:
                if 0 <= step - delay < CHUNKS:
                    stage(step - delay)

    def consume(xg, gain, total, load_weights, k):
        @pl.loop(0, tiles)
        def _(j):
            off = pl.multiple_of(j * tile, tile)
            block = xg[k, :, :, pl.ds(off, tile)].astype(F32)
            part_sq = squares[...]
            added = None
            for h in (0, 1):
                rows = block[:, 8 * h : 8 * h + 8, :].reshape(8 * width, tile)
                for i in range(tile // 128):
                    piece = rows[:, 128 * i : 128 * (i + 1)]
                    part_sq = part_sq + piece * piece
                at = pl.multiple_of(h * half + k * cw + off, tile)
                scaled = (rows * gain[:, pl.ds(at, tile)]).astype(BF16)
                product = jnp.dot(scaled, load_weights(pl.ds(at, tile)), preferred_element_type=F32)
                added = product if added is None else added + product
            squares[...] = part_sq
            total[...] += added

    def inverse_norm():
        mean_square = jnp.sum(squares[...], axis=1, keepdims=True) * (1.0 / features)
        return lax.rsqrt(mean_square + 1e-05)

    own, along, over, last = gather_stages(0, xg1)

    def project(k):
        if k == 0:
            for copy in weights[:3]:
                copy.wait()
        last(k)
        consume(
            xg1, gain_in, acc,
            lambda rows: jnp.concatenate([wq[rows, :], wk[rows, :], wv[rows, :]], axis=1), k,
        )

    run([(0, own), (1, along(1)), (1, over(0)), (2, along(2)), (2, over(1)), (3, along(3)),
         (3, over(2)), (4, over(3)), (5, project)])

    scale = inverse_norm()
    squares[...] = jnp.zeros_like(squares)
    raw = acc[...] * scale
    queries = raw[:, :128]
    kv = raw[:, 128:].astype(BF16)
    out_row = lax.broadcasted_iota(jnp.int32, (128, 128), 0)
    in_col = lax.broadcasted_iota(jnp.int32, (128, 128), 1)
    wanted = ((out_row // 8) % 2) * 64 + (out_row % 8) * 8 + out_row // 16
    order = jnp.where(in_col == wanted, 1.0, 0.0).astype(BF16)
    nt = (((1,), (1,)), ((), ()))
    turned = lax.dot_general(order, kv, nt, preferred_element_type=F32)
    kvs[...] = turned.astype(BF16).reshape(KVH, 16, 128)

    def kv_copy(step):
        peer = lax.rem(me + step, width)
        return lambda: remote(
            kvs.at[peer // 2], kvr.at[me], kv_send.at[step], kv_recv.at[me], peer
        )

    for step in range(1, width):
        launch(kv_copy(step))
    kvr[me] = kvs[me // 2]

    token_pos = jnp.broadcast_to(pos[...].astype(F32), (128, 128))
    exponent = lax.broadcasted_iota(jnp.int32, (64, 128), 0).astype(F32)
    inverse = jnp.exp(-math.log(500000.0) * (2.0 * exponent / 128))
    angle = token_pos[:64] * inverse
    cos_t, sin_t = jnp.cos(angle), jnp.sin(angle)
    cosine = jnp.concatenate([cos_t, cos_t], axis=0).T
    sine = jnp.concatenate([-sin_t, sin_t], axis=0).T

    def turn(values):
        return values * cosine + pltpu.roll(values, 64, 1) * sine

    query = turn(queries).astype(BF16)
    row = lax.broadcasted_iota(jnp.int32, (128, 128), 0).astype(F32)
    col = lax.broadcasted_iota(jnp.int32, (128, 128), 1).astype(F32)
    allowed = (row >= col) & (token_pos.T - token_pos == row - col)

    for step in range(1, width):
        source = lax.rem(me + step, width)
        remote(kvs.at[0], kvr.at[source], kv_send.at[step], kv_recv.at[source], sibling).wait_recv()
    both = kvr[...].astype(F32)
    key_t = both[:, 0:8, :].reshape(128, 128)
    value_t = both[:, 8:16, :].reshape(128, 128).astype(BF16)
    first, second = key_t[:64], key_t[64:]
    key_rows = jnp.concatenate(
        [first * cos_t - second * sin_t, second * cos_t + first * sin_t], axis=0
    ).astype(BF16)
    scores = jnp.dot(query, key_rows, preferred_element_type=F32) * (1.0 / math.sqrt(128))
    scores = jnp.where(allowed, scores, -1e30)
    largest = jnp.max(scores, axis=-1, keepdims=True)
    attn = jnp.where(allowed, jnp.exp(scores - largest), 0.0)
    attn = (attn / jnp.sum(attn, axis=-1, keepdims=True)).astype(BF16)
    ctx[...] = lax.dot_general(attn, value_t, nt, preferred_element_type=F32).astype(BF16)

    def tiled(body):
        @pl.loop(0, tiles)
        def _(j):
            body(pl.multiple_of(j * tile, tile))

    def multiply(k):
        if k == 0:
            weights[3].wait()

        def body(off):
            at = pl.multiple_of(k * cw + off, tile)
            one = jnp.dot(ctx[...], wo[:, pl.ds(at, tile)], preferred_element_type=F32)
            at = pl.multiple_of(half + k * cw + off, tile)
            two = jnp.dot(ctx[...], wo[:, pl.ds(at, tile)], preferred_element_type=F32)
            for t in range(width):
                rows = jnp.concatenate([one[8 * t : 8 * t + 8], two[8 * t : 8 * t + 8]], axis=0)
                part[k, t % 2, (t // 2) % 2, t // 4, :, pl.ds(off, tile)] = rows.astype(BF16)

        tiled(body)
        launch(lambda: remote(part.at[k, 1 - c], rb1.at[k], sib_send.at[k], sib_recv.at[k], sibling))

    def sum_cores(k):
        remote(part.at[k, 1 - c], rb1.at[k], sib_send.at[k], sib_recv.at[k], sibling).wait_recv()

        def body(off):
            cols = pl.ds(off, tile)
            s1[k, :, :, cols] = (
                part[k, c, 1 - y, :, :, cols].astype(F32) + rb1[k, 1 - y, :, :, cols].astype(F32)
            ).astype(BF16)

        tiled(body)
        launch(lambda: remote(s1.at[k], rb2.at[k], y_send.at[k], y_recv.at[k], across))

    def sum_across(k):
        remote(s1.at[k], rb2.at[k], y_send.at[k], y_recv.at[k], across).wait_recv()

        def body(off):
            cols = pl.ds(off, tile)
            s2[k, :, :, cols] = (
                part[k, c, y, :, :, cols].astype(F32)
                + rb1[k, y, :, :, cols].astype(F32)
                + rb2[k, :, :, cols].astype(F32)
            )

        tiled(body)

    def up_copy(k, target):
        i = target - 1
        return lambda: remote(
            up_out.at[k, i], up_in.at[k, i], up_send.at[k, i], up_recv.at[k, i], upper
        )

    def down_copy(k, target):
        return lambda: remote(
            down_out.at[k, target], down_in.at[k, target], down_send.at[k, target],
            down_recv.at[k, target], lower,
        )

    def hop(j):
        def stage(k):
            for target in (3, 2, 1):
                if target > j:
                    @pl.when(z == j)
                    def _(target=target):
                        value = s2[k, target]
                        if j > 0:
                            up_copy(k, target)().wait_recv()
                            value = value + up_in[k, target - 1].astype(F32)
                        up_out[k, target - 1] = value.astype(BF16)
                    launch(up_copy(k, target), z == j)
            for target in (0, 1, 2):
                if target < 3 - j:
                    @pl.when(z == 3 - j)
                    def _(target=target):
                        value = s2[k, target]
                        if j > 0:
                            down_copy(k, target)().wait_recv()
                            value = value + down_in[k, target].astype(F32)
                        down_out[k, target] = value.astype(BF16)
                    launch(down_copy(k, target), z == 3 - j)
        return stage

    own2, along2, over2, last2 = gather_stages(1, xg2)

    def finish(k):
        for target in range(4):
            @pl.when(z == target)
            def _(target=target):
                value = s2[k, target]
                if target > 0:
                    up_copy(k, target)().wait_recv()
                    value = value + up_in[k, target - 1].astype(F32)
                if target < 3:
                    down_copy(k, target)().wait_recv()
                    value = value + down_in[k, target].astype(F32)
                s2[k, target] = value
        residual = (s2[k, z] + hidden_rows(k, 0, cw))
        res_out[:, pl.ds(k * cw, cw)] = residual[:8].astype(BF16)
        res_out[:, pl.ds(half + k * cw, cw)] = residual[8:].astype(BF16)
        xg2[k, me] = residual.astype(BF16)
        own2(k)

    def project_next(k):
        if k == 0:
            weights[4].wait()
        last2(k)
        consume(xg2, gain_out, acc_next, lambda rows: wn[rows, :], k)

    run([(0, multiply), (1, sum_cores), (2, sum_across), (2, hop(0)), (3, hop(1)), (4, hop(2)),
         (5, finish), (6, along2(1)), (6, over2(0)), (7, along2(2)), (7, over2(1)), (8, along2(3)),
         (8, over2(2)), (9, over2(3)), (10, project_next)])

    next_out[...] = turn(acc_next[...] * inverse_norm()).astype(BF16)

    for make, when in pending:
        if when is None:
            make().wait_send()
        else:
            pl.when(when)(lambda make=make: make().wait_send())


def fused(hidden, positions, norm_in, w_query, w_key, w_value, w_out, norm_out, w_next):
    share, features = hidden.shape
    tokens = positions.shape[0]
    cw = features // 2 // CHUNKS
    columns = w_query.shape[1]
    vmem = pl.BlockSpec(memory_space=pltpu.VMEM)
    anywhere = pl.BlockSpec(memory_space=pl.ANY)
    dma = pltpu.SemaphoreType.DMA
    return pl.pallas_call(
        block_kernel,
        out_shape=(
            jax.ShapeDtypeStruct((share, features), BF16),
            jax.ShapeDtypeStruct((tokens, columns), BF16),
        ),
        in_specs=[vmem] * 4 + [anywhere] * 5,
        out_specs=(vmem, vmem),
        scratch_shapes=[
            pltpu.VMEM(w_query.shape, BF16),
            pltpu.VMEM(w_key.shape, BF16),
            pltpu.VMEM(w_value.shape, BF16),
            pltpu.VMEM(w_out.shape, BF16),
            pltpu.VMEM(w_next.shape, BF16),
            pltpu.VMEM((CHUNKS, 16, 16, cw), BF16),
            pltpu.VMEM((CHUNKS, 16, 16, cw), BF16),
            pltpu.VMEM((CHUNKS, 2, 2, 4, 16, cw), BF16),
            pltpu.VMEM((CHUNKS, 2, 4, 16, cw), BF16),
            pltpu.VMEM((CHUNKS, 4, 16, cw), BF16),
            pltpu.VMEM((CHUNKS, 4, 16, cw), BF16),
            pltpu.VMEM((CHUNKS, 4, 16, cw), F32),
            pltpu.VMEM((CHUNKS, 3, 16, cw), BF16),
            pltpu.VMEM((CHUNKS, 3, 16, cw), BF16),
            pltpu.VMEM((CHUNKS, 3, 16, cw), BF16),
            pltpu.VMEM((CHUNKS, 3, 16, cw), BF16),
            pltpu.VMEM((KVH, 16, 128), BF16),
            pltpu.VMEM((16, 16, 128), BF16),
            pltpu.VMEM((tokens, 256), F32),
            pltpu.VMEM((tokens, columns), F32),
            pltpu.VMEM((tokens, 128), F32),
            pltpu.VMEM((tokens, 128), BF16),
            dma((5,)),
            dma((2, CHUNKS, 29)),
            dma((2, CHUNKS, 16)),
            dma((16,)),
            dma((16,)),
            dma((CHUNKS,)),
            dma((CHUNKS,)),
            dma((CHUNKS,)),
            dma((CHUNKS,)),
            dma((CHUNKS, 3)),
            dma((CHUNKS, 3)),
            dma((CHUNKS, 3)),
            dma((CHUNKS, 3)),
        ],
        compiler_params=pltpu.CompilerParams(
            collective_id=0, has_side_effects=True, vmem_limit_bytes=56 * 1024 * 1024
        ),
        name="attention_block",
    )(
        hidden, positions.reshape(1, tokens), norm_in.reshape(1, features),
        norm_out.reshape(1, features), w_query, w_key, w_value, w_out, w_next,
    )


def fits(hidden, positions, w_query, w_key):
    return (
        lax.axis_size("tensor") == 16
        and hidden.shape[0] == 8
        and positions.shape[0] == 128
        and w_query.shape[1] == 128
        and w_key.shape[1] == 64
        and hidden.shape[1] % (2 * CHUNKS * 128) == 0
    )


def on_device(hidden, positions, norm_in, w_query, w_key, w_value, w_out, norm_out, w_next):
    if fits(hidden, positions, w_query, w_key):
        return fused(
            hidden, positions, norm_in, w_query, w_key, w_value, w_out, norm_out, w_next
        )
    width = lax.axis_size("tensor")
    tokens = positions.shape[0]
    share = hidden.shape[0]
    features = hidden.shape[1]
    head_dim = w_query.shape[1]
    key_cols = w_key.shape[1]
    residual = hidden.astype(jnp.float32)
    x_in = normalize(residual, norm_in).astype(jnp.bfloat16)
    w_input = jnp.concatenate([w_query, w_key, w_value], axis=1)
    projected = jnp.dot(
        lax.all_gather(x_in, "tensor", axis=0, tiled=True),
        w_input,
        preferred_element_type=jnp.float32,
    )
    queries = rotary(projected[:, :head_dim], positions, head_dim).astype(jnp.bfloat16)
    key_raw = projected[:, head_dim : head_dim + key_cols].astype(jnp.bfloat16)
    value_local = projected[:, head_dim + key_cols :].astype(jnp.bfloat16)
    local = jnp.stack([key_raw, value_local], axis=0).reshape(2, tokens, key_cols // KVH, KVH)
    per_group = jnp.transpose(local, (3, 0, 1, 2))
    sent = jnp.repeat(per_group, width // KVH, axis=0)
    pairs = lax.all_to_all(sent, "tensor", split_axis=0, concat_axis=0, tiled=True)
    pairs = jnp.transpose(pairs, (1, 2, 0, 3)).reshape(2, tokens, head_dim)
    key_block = rotary(pairs[0].astype(jnp.float32), positions, head_dim).astype(jnp.bfloat16)
    value_block = pairs[1]
    context = attend(queries, key_block, value_block, positions)
    packed = jnp.dot(context, w_out, preferred_element_type=jnp.float32).astype(jnp.bfloat16)
    received = lax.all_to_all(packed, "tensor", split_axis=0, concat_axis=0, tiled=True)
    mixed = jnp.sum(received.reshape(width, share, features).astype(jnp.float32), axis=0)
    residual_f = residual + mixed
    residual_out = residual_f.astype(jnp.bfloat16)
    x_next = normalize(residual_f, norm_out).astype(jnp.bfloat16)
    next_raw = jnp.dot(
        lax.all_gather(x_next, "tensor", axis=0, tiled=True),
        w_next,
        preferred_element_type=jnp.float32,
    )
    query_next = rotary(next_raw, positions, head_dim).astype(jnp.bfloat16)
    return (residual_out, query_next)


def solution(mesh):
    placed = (
        P(("groups", "tensor"), None),
        P("groups"),
        P(),
        P(None, "tensor"),
        P(None, "tensor"),
        P(None, "tensor"),
        P("tensor", None),
        P(),
        P(None, "tensor"),
    )
    return jax.shard_map(
        on_device,
        mesh=mesh,
        in_specs=placed,
        out_specs=(P(("groups", "tensor"), None), P("groups", "tensor")),
        check_vma=False,
    )
```

time: 328 us -> 119 us (0.36)
  waiting for transfers between devices: 188 us -> 0 us
  Pallas kernels: 0 us -> 107 us
  blocking collectives: 37.7 us -> 0 us
  matrix products: 30.9 us -> 0 us
  other arithmetic: 18.6 us -> 0 us
  local copies, waits for them, and re-layouts: 27.5 us -> 11.1 us
  between operations: 14.3 us -> 0.65 us
  starting transfers between devices: 9.78 us -> 0 us
    all_gather x2 -> x0, waiting for transfers between devices: 111 us -> none  [the longest x1 65.6 us: on_device(): lax.all_gather(x_next, 'tensor', axis=0, tiled=True)]
    pallas_call x0 -> x1, Pallas kernels: none -> 107 us  [fused(): pl.pallas_call(block_kernel, out_shape=(jax.ShapeDtypeStruct((share, feat...]
    all_to_all x2 -> x0, waiting for transfers between devices: 77.4 us -> none  [the longest x1 77.4 us: on_device(): lax.all_to_all(packed, 'tensor', split_axis=0, concat_axis=0, tiled=True)]
    all_gather x2 -> x0, blocking collectives: 37.7 us -> none  [the longest x1 19.6 us: on_device(): lax.all_gather(key_raw, 'tensor', axis=1, tiled=True)]
    dot_general x6 -> x0, matrix products: 30.9 us -> none  [the longest x2 10.7 us: rotate(): jnp.einsum('...bk,kl->...bl', shaped, table, precision=lax.Precision.HIGH...]
    convert_element_type x7 -> x0, other arithmetic: 11.7 us -> none  [the longest x1 6.74 us: on_device(): (shaped / scale[:, :, None]).astype(jnp.bfloat16).reshape(tokens, features)]
    all_to_all x2 -> x0, starting transfers between devices: 9.7 us -> none  [the longest x1 6.02 us: on_device(): lax.all_to_all(packed, 'tensor', split_axis=0, concat_axis=0, tiled=True)]
    all_to_all x1 -> x0, local copies, waits for them, and re-layouts: 7.36 us -> none  [on_device(): lax.all_to_all(packed, 'tensor', split_axis=0, concat_axis=0, tiled=True)]
  transfers between devices with their start and end apart: 4 -> 0, of which waited for: 3 -> 0; matrix products, arithmetic and copies ran while one was open for 7% -> 0% of each run, Pallas kernels for 0% -> 0%
where the time goes in v1:
time: 119 us; the launch traced here: 118 us
  Pallas kernels  107 us (90%)
  local copies, waits for them, and re-layouts  11.1 us (9%)
    pallas_call x1, Pallas kernels, fused(): pl.pallas_call(block_kernel, out_shape=(jax.ShapeDtypeStruct((share, feat...  107 us
    unnamed x6, local copies, waits for them, and re-layouts  11.1 us

profile of v1, /device:TPU:0, one launch (start us, length us, event | category | flops | bytes accessed | tf_op | source)
XLA Modules:
  0.0 118.3 jit_solution(2978701243951308221)
XLA Ops:
  0.6 0.0 copy-start
  0.6 4.9 %copy.11.wk_hbm = bf16[16384,64]{1,0:T(8,128)(2,1)} copy(bf16[16384,64]{0,1:T(8,128)(2,1)} %param.13) | data formatting | bytes 4194304 | tf_op args[4]
  5.6 0.0 copy-done
  5.6 3.2 %copy.12.wv_hbm = bf16[16384,64]{1,0:T(8,128)(2,1)} copy(bf16[16384,64]{0,1:T(8,128)(2,1)S(1)} %copy-done) | data formatting | bytes 4194304 | tf_op args[5]
  8.7 106.6 %attention_block.1 = (bf16[8,16384]{1,0:T(8,128)(2,1)}, bf16[128,128]{1,0:T(8,128)(2,1)}) custom-call(bf16[8,16384]{1,0:T(8,128)(2,1)} %hid.1, s32[1,128]{1,0:T(1,128)} %bitcast.5, f32[1,16384]{1,0:T(1,128)} %bitcast.3, f32[1,16384]{1,0:T(1,128)} %bitcast.4, bf16[16384,128]{1,0:T(8,128)(2,1)} %wq_hbm.1, bf16[16384,64]{1,0:T(8,128)(2,1)} %copy.11.wk_hbm, ...), custom_call_target="tpu_custom_call" | custom-call | tf_op jit(solution)/shard_map/attention_block/pallas_call | solution.py:404
  115.3 1.7 %copy.15 = bf16[8,16384]{1,0:T(8,128)(2,1)} copy(bf16[8,16384]{1,0:T(8,128)(2,1)} %get-tuple-element.4) | data formatting | bytes 524288
  117.0 1.4 %copy.16 = bf16[128,128]{1,0:T(8,128)(2,1)} copy(bf16[128,128]{1,0:T(8,128)(2,1)} %get-tuple-element.5) | data formatting | bytes 65536
Async XLA Ops:
  0.6 4.9 %copy-start = (bf16[16384,64]{0,1:T(8,128)(2,1)S(1)}, bf16[16384,64]{0,1:T(8,128)(2,1)}, u32[]{:S(2)}) copy-start(bf16[16384,64]{0,1:T(8,128)(2,1)} %param.14) | copy-start | bytes 6291460

commit v2 on v1

--- a/solution.py
+++ b/solution.py
@@ -54,7 +54,7 @@
 def block_kernel(
     hid, pos, gain_in, gain_out, wq_hbm, wk_hbm, wv_hbm, wo_hbm, wn_hbm,
     res_out, next_out,
-    wq, wk, wv, wo, wn, xg1, xg2, part, rb1, s1, rb2, s2, up_out, up_in, down_out, down_in,
+    wq, wkv, wo, wn, xg1, xg2, part, rb1, s1, rb2, s2, up_out, up_in, down_out, down_in,
     kvs, kvr, acc, acc_next, squares, ctx,
     w_sem, ag_send, ag_recv, kv_send, kv_recv, sib_send, sib_recv, y_send, y_recv,
     up_send, up_recv, down_send, down_recv,
@@ -64,6 +64,8 @@
     width = 16
     features = hid.shape[1]
     half = features // 2
+    key_cols = wk_hbm.shape[0]
+    nt = (((1,), (1,)), ((), ()))
     cw = half // CHUNKS
     tile = min(512, cw)
     tiles = cw // tile
@@ -91,7 +93,7 @@
     weights = [
         pltpu.make_async_copy(src, dst, w_sem.at[i])
         for i, (src, dst) in enumerate(
-            [(wq_hbm, wq), (wk_hbm, wk), (wv_hbm, wv), (wo_hbm, wo), (wn_hbm, wn)]
+            [(wq_hbm, wq), (wk_hbm, wkv.at[:key_cols]), (wv_hbm, wkv.at[key_cols:]), (wo_hbm, wo), (wn_hbm, wn)]
         )
     ]
     for copy in weights:
@@ -178,13 +180,12 @@
                 if 0 <= step - delay < CHUNKS:
                     stage(step - delay)
 
-    def consume(xg, gain, total, load_weights, k):
+    def consume(xg, gain, add, k):
         @pl.loop(0, tiles)
         def _(j):
             off = pl.multiple_of(j * tile, tile)
             block = xg[k, :, :, pl.ds(off, tile)].astype(F32)
             part_sq = squares[...]
-            added = None
             for h in (0, 1):
                 rows = block[:, 8 * h : 8 * h + 8, :].reshape(8 * width, tile)
                 for i in range(tile // 128):
@@ -192,26 +193,25 @@
                     part_sq = part_sq + piece * piece
                 at = pl.multiple_of(h * half + k * cw + off, tile)
                 scaled = (rows * gain[:, pl.ds(at, tile)]).astype(BF16)
-                product = jnp.dot(scaled, load_weights(pl.ds(at, tile)), preferred_element_type=F32)
-                added = product if added is None else added + product
+                add(scaled, pl.ds(at, tile))
             squares[...] = part_sq
-            total[...] += added
 
     def inverse_norm():
         mean_square = jnp.sum(squares[...], axis=1, keepdims=True) * (1.0 / features)
         return lax.rsqrt(mean_square + 1e-05)
 
     own, along, over, last = gather_stages(0, xg1)
+
+    def add_projections(scaled, at):
+        acc[:, :128] += jnp.dot(scaled, wq[at, :], preferred_element_type=F32)
+        acc[:, 128:] += lax.dot_general(scaled, wkv[:, at], nt, preferred_element_type=F32)
 
     def project(k):
         if k == 0:
             for copy in weights[:3]:
                 copy.wait()
         last(k)
-        consume(
-            xg1, gain_in, acc,
-            lambda rows: jnp.concatenate([wq[rows, :], wk[rows, :], wv[rows, :]], axis=1), k,
-        )
+        consume(xg1, gain_in, add_projections, k)
 
     run([(0, own), (1, along(1)), (1, over(0)), (2, along(2)), (2, over(1)), (3, along(3)),
          (3, over(2)), (4, over(3)), (5, project)])
@@ -225,7 +225,6 @@
     in_col = lax.broadcasted_iota(jnp.int32, (128, 128), 1)
     wanted = ((out_row // 8) % 2) * 64 + (out_row % 8) * 8 + out_row // 16
     order = jnp.where(in_col == wanted, 1.0, 0.0).astype(BF16)
-    nt = (((1,), (1,)), ((), ()))
     turned = lax.dot_general(order, kv, nt, preferred_element_type=F32)
     kvs[...] = turned.astype(BF16).reshape(KVH, 16, 128)
 
@@ -374,11 +373,14 @@
         xg2[k, me] = residual.astype(BF16)
         own2(k)
 
+    def add_next(scaled, at):
+        acc_next[...] += jnp.dot(scaled, wn[at, :], preferred_element_type=F32)
+
     def project_next(k):
         if k == 0:
             weights[4].wait()
         last2(k)
-        consume(xg2, gain_out, acc_next, lambda rows: wn[rows, :], k)
+        consume(xg2, gain_out, add_next, k)
 
     run([(0, multiply), (1, sum_cores), (2, sum_across), (2, hop(0)), (3, hop(1)), (4, hop(2)),
          (5, finish), (6, along2(1)), (6, over2(0)), (7, along2(2)), (7, over2(1)), (8, along2(3)),
@@ -411,8 +413,7 @@
         out_specs=(vmem, vmem),
         scratch_shapes=[
             pltpu.VMEM(w_query.shape, BF16),
-            pltpu.VMEM(w_key.shape, BF16),
-            pltpu.VMEM(w_value.shape, BF16),
+            pltpu.VMEM((2 * w_key.shape[1], features), BF16),
             pltpu.VMEM(w_out.shape, BF16),
             pltpu.VMEM(w_next.shape, BF16),
             pltpu.VMEM((CHUNKS, 16, 16, cw), BF16),
@@ -452,7 +453,7 @@
         name="attention_block",
     )(
         hidden, positions.reshape(1, tokens), norm_in.reshape(1, features),
-        norm_out.reshape(1, features), w_query, w_key, w_value, w_out, w_next,
+        norm_out.reshape(1, features), w_query, w_key.T, w_value.T, w_out, w_next,
     )
 
 

time: 119 us -> 110 us (0.924)
  local copies, waits for them, and re-layouts: 11.1 us -> 3.04 us
    unnamed x6 -> x2, local copies, waits for them, and re-layouts: 11.1 us -> 3.04 us
where the time goes in v2:
time: 110 us
  Pallas kernels  107 us (97%)
  local copies, waits for them, and re-layouts  3.04 us (3%)
    pallas_call x1, Pallas kernels, fused(): pl.pallas_call(block_kernel, out_shape=(jax.ShapeDtypeStruct((share, feat...  107 us
    unnamed x2, local copies, waits for them, and re-layouts  3.04 us

profile of v2, /device:TPU:0, one launch (start us, length us, event | category | flops | bytes accessed | tf_op | source)
XLA Modules:
  0.0 110.2 jit_solution(12741043143277765057)
XLA Ops:
  0.6 106.5 %attention_block.1 = (bf16[8,16384]{1,0:T(8,128)(2,1)}, bf16[128,128]{1,0:T(8,128)(2,1)}) custom-call(bf16[8,16384]{1,0:T(8,128)(2,1)} %hid.1, s32[1,128]{1,0:T(1,128)} %bitcast.9, f32[1,16384]{1,0:T(1,128)} %bitcast.7, f32[1,16384]{1,0:T(1,128)} %bitcast.8, bf16[16384,128]{1,0:T(8,128)(2,1)} %wq_hbm.1, bf16[64,16384]{1,0:T(8,128)(2,1)} %bitcast.5, ...), custom_call_target="tpu_custom_call" | custom-call | tf_op jit(solution)/shard_map/attention_block/pallas_call | solution.py:406
  107.2 1.7 %copy.13 = bf16[8,16384]{1,0:T(8,128)(2,1)} copy(bf16[8,16384]{1,0:T(8,128)(2,1)} %get-tuple-element.4) | data formatting | bytes 524288
  108.8 1.4 %copy.14 = bf16[128,128]{1,0:T(8,128)(2,1)} copy(bf16[128,128]{1,0:T(8,128)(2,1)} %get-tuple-element.5) | data formatting | bytes 65536

commit v3 on v2

--- a/solution.py
+++ b/solution.py
@@ -56,7 +56,7 @@
     res_out, next_out,
     wq, wkv, wo, wn, xg1, xg2, part, rb1, s1, rb2, s2, up_out, up_in, down_out, down_in,
     kvs, kvr, acc, acc_next, squares, ctx,
-    w_sem, ag_send, ag_recv, kv_send, kv_recv, sib_send, sib_recv, y_send, y_recv,
+    w_sem, ag_send, ag_recv, sib_in, kv_send, kv_recv, sib_send, sib_recv, y_send, y_recv,
     up_send, up_recv, down_send, down_recv,
 ):
     me = lax.axis_index("tensor")
@@ -100,11 +100,16 @@
         copy.start()
 
     barrier = pltpu.get_barrier_semaphore()
-    for step in range(1, width):
+
+    def greet(device):
         pl.semaphore_signal(
-            barrier, inc=1, device_id={"tensor": lax.rem(me + step, width)},
-            device_id_type=pl.DeviceIdType.MESH,
-        )
+            barrier, inc=1, device_id={"tensor": device}, device_id_type=pl.DeviceIdType.MESH
+        )
+
+    greet(sibling)
+    greet(across)
+    pl.when(z < 3)(lambda: greet(upper))
+    pl.when(z > 0)(lambda: greet(lower))
 
     def hidden_rows(k, off, size):
         first = hid[:, pl.ds(k * cw + off, size)].astype(F32)
@@ -116,63 +121,82 @@
     acc[...] = jnp.zeros_like(acc)
     acc_next[...] = jnp.zeros_like(acc_next)
     squares[...] = jnp.zeros_like(squares)
-    pl.semaphore_wait(barrier, width - 1)
+    inner = (z > 0) & (z < 3)
+    pl.when(inner)(lambda: pl.semaphore_wait(barrier, 4))
+    pl.when(jnp.logical_not(inner))(lambda: pl.semaphore_wait(barrier, 3))
 
     def gather_stages(a, xg):
-        def copy(k, origin, slot, device):
-            return lambda: remote(
-                xg.at[k, origin], xg.at[k, origin], ag_send.at[a, k, slot], ag_recv.at[a, k, origin], device
+        def copy(k, origin, way, device):
+            arrival = sib_in.at[a, k] if way == 3 else ag_recv.at[a, k, origin]
+            return remote(
+                xg.at[k, origin], xg.at[k, origin], ag_send.at[a, k, way], arrival, device
             )
 
+        def blocks(k, count, way):
+            return remote(
+                xg.at[k, pl.ds(0, count)], xg.at[k, pl.ds(0, count)],
+                ag_send.at[a, k, way], sib_in.at[a, k], sibling,
+            )
+
         def arrived(k, origin):
-            copy(k, origin, 0, sibling)().wait_recv()
+            copy(k, origin, 0, sibling).wait_recv()
 
         def own(k):
-            launch(copy(k, me, 0, upper), z < 3)
-            launch(copy(k, me, 1, lower), z > 0)
-            launch(copy(k, me, 2, across))
-            launch(copy(k, me, 3, sibling))
-
-        sides = [(d, s) for d in (1, 2, 3) for s in (0, 1)]
-
-        def where(d, s):
-            return (z - d, z >= d) if s == 0 else (z + d, z + d <= 3)
+            copy(k, me, 2, across).start()
+            pl.when(z < 3)(lambda: copy(k, me, 0, upper).start())
+            pl.when(z > 0)(lambda: copy(k, me, 1, lower).start())
+            copy(k, me, 3, sibling).start()
 
         def along(d):
             def stage(k):
-                for s in (0, 1):
-                    zz, there = where(d, s)
-                    origin = index(zz, y, c)
-                    slot = 4 + 3 * sides.index((d, s))
-                    pl.when(there)(lambda: arrived(k, origin))
-                    launch(copy(k, origin, slot, across), there)
+                @pl.when(z >= d)
+                def _():
+                    origin = index(z - d, y, c)
+                    arrived(k, origin)
+                    copy(k, origin, 2, across).start()
                     if d < 3:
-                        if s == 0:
-                            launch(copy(k, origin, slot + 1, upper), there & (z < 3))
-                        else:
-                            launch(copy(k, origin, slot + 1, lower), there & (z > 0))
-                    launch(copy(k, origin, slot + 2, sibling), there)
+                        pl.when(z < 3)(lambda: copy(k, origin, 0, upper).start())
+                    copy(k, origin, 3, sibling).start()
+
+                @pl.when(z + d <= 3)
+                def _():
+                    origin = index(z + d, y, c)
+                    arrived(k, origin)
+                    copy(k, origin, 2, across).start()
+                    if d < 3:
+                        pl.when(z > 0)(lambda: copy(k, origin, 1, lower).start())
+                    copy(k, origin, 3, sibling).start()
             return stage
 
         def over(d):
+            def pass_on(k, zz):
+                origin = index(zz, 1 - y, c)
+                arrived(k, origin)
+                copy(k, origin, 3, sibling).start()
+
             def stage(k):
                 if d == 0:
-                    origin = index(z, 1 - y, c)
-                    arrived(k, origin)
-                    launch(copy(k, origin, 22, sibling))
-                    return
-                for s in (0, 1):
-                    zz, there = where(d, s)
-                    origin = index(zz, 1 - y, c)
-                    pl.when(there)(lambda: arrived(k, origin))
-                    launch(copy(k, origin, 23 + sides.index((d, s)), sibling), there)
+                    pass_on(k, z)
+                else:
+                    pl.when(z >= d)(lambda: pass_on(k, z - d))
+                    pl.when(z + d <= 3)(lambda: pass_on(k, z + d))
             return stage
 
         def last(k):
-            for j in range(8):
-                arrived(k, j * 2 + 1 - c)
-
-        return own, along, over, last
+            blocks(k, 8, 3).wait_recv()
+
+        def sent(k):
+            blocks(k, 4, 2).wait_send()
+            blocks(k, 8, 3).wait_send()
+            for at in range(4):
+                @pl.when(z == at)
+                def _(at=at):
+                    if at < 3:
+                        blocks(k, at + 1, 0).wait_send()
+                    if at > 0:
+                        blocks(k, 4 - at, 1).wait_send()
+
+        return own, along, over, last, sent
 
     def run(stages):
         for step in range(CHUNKS + max(delay for delay, _ in stages)):
@@ -200,7 +224,7 @@
         mean_square = jnp.sum(squares[...], axis=1, keepdims=True) * (1.0 / features)
         return lax.rsqrt(mean_square + 1e-05)
 
-    own, along, over, last = gather_stages(0, xg1)
+    own, along, over, last, sent = gather_stages(0, xg1)
 
     def add_projections(scaled, at):
         acc[:, :128] += jnp.dot(scaled, wq[at, :], preferred_element_type=F32)
@@ -237,6 +261,9 @@
     for step in range(1, width):
         launch(kv_copy(step))
     kvr[me] = kvs[me // 2]
+
+    for k in range(CHUNKS):
+        sent(k)
 
     token_pos = jnp.broadcast_to(pos[...].astype(F32), (128, 128))
     exponent = lax.broadcasted_iota(jnp.int32, (64, 128), 0).astype(F32)
@@ -340,7 +367,8 @@
                             up_copy(k, target)().wait_recv()
                             value = value + up_in[k, target - 1].astype(F32)
                         up_out[k, target - 1] = value.astype(BF16)
-                    launch(up_copy(k, target), z == j)
+                        up_copy(k, target)().start()
+                    pending.append((up_copy(k, target), z == j))
             for target in (0, 1, 2):
                 if target < 3 - j:
                     @pl.when(z == 3 - j)
@@ -350,10 +378,18 @@
                             down_copy(k, target)().wait_recv()
                             value = value + down_in[k, target].astype(F32)
                         down_out[k, target] = value.astype(BF16)
-                    launch(down_copy(k, target), z == 3 - j)
+                        down_copy(k, target)().start()
+                    pending.append((down_copy(k, target), z == 3 - j))
         return stage
 
-    own2, along2, over2, last2 = gather_stages(1, xg2)
+    def drain():
+        for make, when in pending:
+            if when is None:
+                make().wait_send()
+            else:
+                pl.when(when)(lambda make=make: make().wait_send())
+
+    own2, along2, over2, last2, sent2 = gather_stages(1, xg2)
 
     def finish(k):
         for target in range(4):
@@ -379,6 +415,8 @@
     def project_next(k):
         if k == 0:
             weights[4].wait()
+        if k == CHUNKS - 1:
+            drain()
         last2(k)
         consume(xg2, gain_out, add_next, k)
 
@@ -388,11 +426,8 @@
 
     next_out[...] = turn(acc_next[...] * inverse_norm()).astype(BF16)
 
-    for make, when in pending:
-        if when is None:
-            make().wait_send()
-        else:
-            pl.when(when)(lambda make=make: make().wait_send())
+    for k in range(CHUNKS):
+        sent2(k)
 
 
 def fused(hidden, positions, norm_in, w_query, w_key, w_value, w_out, norm_out, w_next):
@@ -434,8 +469,9 @@
             pltpu.VMEM((tokens, 128), F32),
             pltpu.VMEM((tokens, 128), BF16),
             dma((5,)),
-            dma((2, CHUNKS, 29)),
+            dma((2, CHUNKS, 4)),
             dma((2, CHUNKS, 16)),
+            dma((2, CHUNKS)),
             dma((16,)),
             dma((16,)),
             dma((CHUNKS,)),

time: 110 us -> 106 us (0.964)
  Pallas kernels: 107 us -> 103 us
    pallas_call x1, Pallas kernels: 107 us -> 103 us  [fused(): pl.pallas_call(block_kernel, out_shape=(jax.ShapeDtypeStruct((share, feat...]
where the time goes in v3:
time: 106 us
  Pallas kernels  103 us (97%)
  local copies, waits for them, and re-layouts  3.04 us (3%)
    pallas_call x1, Pallas kernels, fused(): pl.pallas_call(block_kernel, out_shape=(jax.ShapeDtypeStruct((share, feat...  103 us
    unnamed x2, local copies, waits for them, and re-layouts  3.04 us

profile of v3, /device:TPU:0, one launch (start us, length us, event | category | flops | bytes accessed | tf_op | source)
XLA Modules:
  0.0 106.2 jit_solution(12704828001771072899)
XLA Ops:
  0.6 102.5 %attention_block.1 = (bf16[8,16384]{1,0:T(8,128)(2,1)}, bf16[128,128]{1,0:T(8,128)(2,1)}) custom-call(bf16[8,16384]{1,0:T(8,128)(2,1)} %hid.1, s32[1,128]{1,0:T(1,128)} %bitcast.9, f32[1,16384]{1,0:T(1,128)} %bitcast.7, f32[1,16384]{1,0:T(1,128)} %bitcast.8, bf16[16384,128]{1,0:T(8,128)(2,1)} %wq_hbm.1, bf16[64,16384]{1,0:T(8,128)(2,1)} %bitcast.5, ...), custom_call_target="tpu_custom_call" | custom-call | tf_op jit(solution)/shard_map/attention_block/pallas_call | solution.py:441
  103.2 1.7 %copy.13 = bf16[8,16384]{1,0:T(8,128)(2,1)} copy(bf16[8,16384]{1,0:T(8,128)(2,1)} %get-tuple-element.4) | data formatting | bytes 524288
  104.9 1.4 %copy.14 = bf16[128,128]{1,0:T(8,128)(2,1)} copy(bf16[128,128]{1,0:T(8,128)(2,1)} %get-tuple-element.5) | data formatting | bytes 65536

commit v4 on v3

--- a/solution.py
+++ b/solution.py
@@ -8,7 +8,41 @@
 from jax.sharding import PartitionSpec as P
 
 KVH = 8
-CHUNKS = 4
+CHUNKS = 8
+FIRST_Y = (6,)
+NEXT_Y = (7,)
+SUM_Z = (0,)
+ORDER_FIRST = (
+    ("own", 0), ("own", 2), ("own", 7), ("own", 5), ("own", 1), ("own", 4), ("own", 3), ("own", 6),
+    ("along1", 2), ("along1", 1), ("over0", 2), ("along1", 4), ("along1", 0), ("along1", 3), ("over0", 1),
+    ("along2", 2), ("over0", 4), ("over0", 0), ("pre", 6), ("along2", 1), ("along2", 4), ("along2", 0),
+    ("over1", 2), ("over1", 4), ("over0", 3), ("along2", 3), ("along1", 5), ("along3", 2), ("along3", 4),
+    ("along1", 7), ("over1", 1), ("over1", 0), ("along1", 6), ("over2", 2), ("along3", 1), ("over1", 3),
+    ("over0", 5), ("along3", 3), ("along3", 0), ("along2", 5), ("over2", 4), ("over0", 7), ("along2", 7),
+    ("over3", 2), ("over2", 1), ("last", 2), ("over2", 3), ("over2", 0), ("along2", 6), ("over3", 4),
+    ("over3", 3), ("over1", 5), ("over1", 7), ("along3", 5), ("over3", 0), ("along3", 7), ("last", 3),
+    ("over3", 1), ("last", 0), ("last", 4), ("along3", 6), ("over2", 7), ("over2", 5), ("over3", 5),
+    ("last", 1), ("over3", 7), ("last", 6), ("last", 5), ("last", 7),
+)
+ORDER_NEXT = (
+    ("mult", 1), ("mult", 0), ("sumc", 1), ("sumc", 0), ("mult", 2), ("hop0", 0), ("sumc", 2), ("mult", 4),
+    ("mult", 7), ("mult", 3), ("sumc", 3), ("suma", 1), ("hop1", 0), ("sumc", 4), ("mult", 5), ("hop0", 1),
+    ("hop2", 0), ("mult", 6), ("hop1", 1), ("suma", 2), ("hop0", 2), ("suma", 3), ("hop0", 3), ("yfin", 0),
+    ("hop1", 2), ("sumc", 5), ("fin", 0), ("hop1", 3), ("suma", 4), ("hop2", 1), ("own", 0), ("sumc", 6),
+    ("sumc", 7), ("hop2", 2), ("hop0", 4), ("fin", 1), ("own", 1), ("hop2", 3), ("suma", 5), ("hop0", 5),
+    ("hop1", 4), ("fin", 2), ("along1", 0), ("own", 2), ("hop2", 4), ("along1", 1), ("suma", 6),
+    ("hop0", 6), ("over0", 0), ("hop1", 5), ("fin", 3), ("along2", 0), ("own", 3), ("suma", 7), ("hop0", 7),
+    ("hop1", 6), ("hop2", 5), ("along1", 2), ("hop2", 6), ("hop1", 7), ("over1", 0), ("over0", 1),
+    ("over0", 2), ("along2", 1), ("over1", 1), ("along3", 0), ("fin", 5), ("own", 5), ("fin", 4),
+    ("own", 4), ("hop2", 7), ("along3", 1), ("fin", 6), ("along2", 2), ("along1", 3), ("own", 6),
+    ("over0", 3), ("fin", 7), ("over2", 1), ("own", 7), ("along1", 4), ("along2", 3), ("over1", 2),
+    ("along1", 5), ("over2", 0), ("along1", 6), ("over1", 3), ("over0", 4), ("along3", 2), ("over0", 5),
+    ("over0", 6), ("pre", 7), ("over3", 1), ("along2", 4), ("along2", 6), ("over3", 0), ("over1", 4),
+    ("along3", 3), ("over2", 3), ("last", 1), ("along2", 5), ("along1", 7), ("over2", 2), ("over1", 6),
+    ("along3", 4), ("last", 0), ("over3", 2), ("over1", 5), ("along3", 6), ("along3", 5), ("along2", 7),
+    ("over2", 4), ("over3", 4), ("over2", 5), ("over3", 3), ("last", 2), ("last", 4), ("over2", 6),
+    ("over3", 5), ("along3", 7), ("over3", 6), ("last", 3), ("last", 5), ("last", 7), ("last", 6),
+)
 F32 = jnp.float32
 BF16 = jnp.bfloat16
 
@@ -125,7 +159,7 @@
     pl.when(inner)(lambda: pl.semaphore_wait(barrier, 4))
     pl.when(jnp.logical_not(inner))(lambda: pl.semaphore_wait(barrier, 3))
 
-    def gather_stages(a, xg):
+    def gather_stages(a, xg, y_first):
         def copy(k, origin, way, device):
             arrival = sib_in.at[a, k] if way == 3 else ag_recv.at[a, k, origin]
             return remote(
@@ -147,8 +181,36 @@
             pl.when(z > 0)(lambda: copy(k, me, 1, lower).start())
             copy(k, me, 3, sibling).start()
 
+        def early(k):
+            if k in y_first:
+                origin = index(z, 1 - y, c)
+                arrived(k, origin)
+                pl.when(z < 3)(lambda: copy(k, origin, 0, upper).start())
+                pl.when(z > 0)(lambda: copy(k, origin, 1, lower).start())
+                copy(k, origin, 3, sibling).start()
+
         def along(d):
+            def both(k):
+                for yy in (y, 1 - y):
+                    @pl.when(z >= d)
+                    def _(origin=index(z - d, yy, c)):
+                        arrived(k, origin)
+                        if d < 3:
+                            pl.when(z < 3)(lambda: copy(k, origin, 0, upper).start())
+                        copy(k, origin, 3, sibling).start()
+
+                    @pl.when(z + d <= 3)
+                    def _(origin=index(z + d, yy, c)):
+                        arrived(k, origin)
+                        if d < 3:
+                            pl.when(z > 0)(lambda: copy(k, origin, 1, lower).start())
+                        copy(k, origin, 3, sibling).start()
+
             def stage(k):
+                if k in y_first:
+                    both(k)
+                    return
+
                 @pl.when(z >= d)
                 def _():
                     origin = index(z - d, y, c)
@@ -175,6 +237,8 @@
                 copy(k, origin, 3, sibling).start()
 
             def stage(k):
+                if k in y_first:
+                    return
                 if d == 0:
                     pass_on(k, z)
                 else:
@@ -186,23 +250,22 @@
             blocks(k, 8, 3).wait_recv()
 
         def sent(k):
-            blocks(k, 4, 2).wait_send()
+            spread = 2 if k in y_first else 1
+            blocks(k, 1 if k in y_first else 4, 2).wait_send()
             blocks(k, 8, 3).wait_send()
             for at in range(4):
                 @pl.when(z == at)
                 def _(at=at):
                     if at < 3:
-                        blocks(k, at + 1, 0).wait_send()
+                        blocks(k, spread * (at + 1), 0).wait_send()
                     if at > 0:
-                        blocks(k, 4 - at, 1).wait_send()
-
-        return own, along, over, last, sent
-
-    def run(stages):
-        for step in range(CHUNKS + max(delay for delay, _ in stages)):
-            for delay, stage in stages:
-                if 0 <= step - delay < CHUNKS:
-                    stage(step - delay)
+                        blocks(k, spread * (4 - at), 1).wait_send()
+
+        return own, early, along, over, last, sent
+
+    def run(stages, order):
+        for name, k in order:
+            stages[name](k)
 
     def consume(xg, gain, add, k):
         @pl.loop(0, tiles)
@@ -224,21 +287,23 @@
         mean_square = jnp.sum(squares[...], axis=1, keepdims=True) * (1.0 / features)
         return lax.rsqrt(mean_square + 1e-05)
 
-    own, along, over, last, sent = gather_stages(0, xg1)
+    own, early, along, over, last, sent = gather_stages(0, xg1, FIRST_Y)
 
     def add_projections(scaled, at):
         acc[:, :128] += jnp.dot(scaled, wq[at, :], preferred_element_type=F32)
         acc[:, 128:] += lax.dot_general(scaled, wkv[:, at], nt, preferred_element_type=F32)
 
+    first_used = [k for name, k in ORDER_FIRST if name == "last"][0]
+
     def project(k):
-        if k == 0:
+        if k == first_used:
             for copy in weights[:3]:
                 copy.wait()
         last(k)
         consume(xg1, gain_in, add_projections, k)
 
-    run([(0, own), (1, along(1)), (1, over(0)), (2, along(2)), (2, over(1)), (3, along(3)),
-         (3, over(2)), (4, over(3)), (5, project)])
+    run(dict(own=own, pre=early, along1=along(1), along2=along(2), along3=along(3), over0=over(0),
+             over1=over(1), over2=over(2), over3=over(3), last=project), ORDER_FIRST)
 
     scale = inverse_norm()
     squares[...] = jnp.zeros_like(squares)
@@ -304,7 +369,7 @@
             body(pl.multiple_of(j * tile, tile))
 
     def multiply(k):
-        if k == 0:
+        if k == ORDER_NEXT[0][1]:
             weights[3].wait()
 
         def body(off):
@@ -324,19 +389,30 @@
 
         def body(off):
             cols = pl.ds(off, tile)
-            s1[k, :, :, cols] = (
+            theirs = (
                 part[k, c, 1 - y, :, :, cols].astype(F32) + rb1[k, 1 - y, :, :, cols].astype(F32)
-            ).astype(BF16)
+            )
+            if k in SUM_Z:
+                s2[1, k, :, :, cols] = theirs
+                s2[0, k, :, :, cols] = (
+                    part[k, c, y, :, :, cols].astype(F32) + rb1[k, y, :, :, cols].astype(F32)
+                )
+            else:
+                s1[k, :, :, cols] = theirs.astype(BF16)
 
         tiled(body)
+        if k in SUM_Z:
+            return
         launch(lambda: remote(s1.at[k], rb2.at[k], y_send.at[k], y_recv.at[k], across))
 
     def sum_across(k):
+        if k in SUM_Z:
+            return
         remote(s1.at[k], rb2.at[k], y_send.at[k], y_recv.at[k], across).wait_recv()
 
         def body(off):
             cols = pl.ds(off, tile)
-            s2[k, :, :, cols] = (
+            s2[0, k, :, :, cols] = (
                 part[k, c, y, :, :, cols].astype(F32)
                 + rb1[k, y, :, :, cols].astype(F32)
                 + rb2[k, :, :, cols].astype(F32)
@@ -344,43 +420,69 @@
 
         tiled(body)
 
-    def up_copy(k, target):
+    def up_copy(k, o, target):
         i = target - 1
         return lambda: remote(
-            up_out.at[k, i], up_in.at[k, i], up_send.at[k, i], up_recv.at[k, i], upper
+            up_out.at[k, o, i], up_in.at[k, o, i], up_send.at[k, o, i], up_recv.at[k, o, i], upper
         )
 
-    def down_copy(k, target):
+    def down_copy(k, o, target):
         return lambda: remote(
-            down_out.at[k, target], down_in.at[k, target], down_send.at[k, target],
-            down_recv.at[k, target], lower,
+            down_out.at[k, o, target], down_in.at[k, o, target], down_send.at[k, o, target],
+            down_recv.at[k, o, target], lower,
         )
 
     def hop(j):
         def stage(k):
-            for target in (3, 2, 1):
-                if target > j:
-                    @pl.when(z == j)
-                    def _(target=target):
-                        value = s2[k, target]
+            for o in (0, 1) if k in SUM_Z else (0,):
+                @pl.when(z == j)
+                def _(o=o):
+                    for target in range(3, j, -1):
+                        value = s2[o, k, target]
                         if j > 0:
-                            up_copy(k, target)().wait_recv()
-                            value = value + up_in[k, target - 1].astype(F32)
-                        up_out[k, target - 1] = value.astype(BF16)
-                        up_copy(k, target)().start()
-                    pending.append((up_copy(k, target), z == j))
-            for target in (0, 1, 2):
-                if target < 3 - j:
-                    @pl.when(z == 3 - j)
-                    def _(target=target):
-                        value = s2[k, target]
+                            up_copy(k, o, target)().wait_recv()
+                            value = value + up_in[k, o, target - 1].astype(F32)
+                        up_out[k, o, target - 1] = value.astype(BF16)
+                        up_copy(k, o, target)().start()
+
+                @pl.when(z == 3 - j)
+                def _(o=o):
+                    for target in range(3 - j):
+                        value = s2[o, k, target]
                         if j > 0:
-                            down_copy(k, target)().wait_recv()
-                            value = value + down_in[k, target].astype(F32)
-                        down_out[k, target] = value.astype(BF16)
-                        down_copy(k, target)().start()
-                    pending.append((down_copy(k, target), z == 3 - j))
+                            down_copy(k, o, target)().wait_recv()
+                            value = value + down_in[k, o, target].astype(F32)
+                        down_out[k, o, target] = value.astype(BF16)
+                        down_copy(k, o, target)().start()
+
+                for target in range(3, j, -1):
+                    pending.append((up_copy(k, o, target), z == j))
+                for target in range(3 - j):
+                    pending.append((down_copy(k, o, target), z == 3 - j))
         return stage
+
+    def whole_line(k, o, then):
+        for target in range(4):
+            @pl.when(z == target)
+            def _(target=target):
+                value = s2[o, k, target]
+                if target > 0:
+                    up_copy(k, o, target)().wait_recv()
+                    value = value + up_in[k, o, target - 1].astype(F32)
+                if target < 3:
+                    down_copy(k, o, target)().wait_recv()
+                    value = value + down_in[k, o, target].astype(F32)
+                then(value)
+
+    def across_copy(k):
+        return lambda: remote(s1.at[k, 0], rb2.at[k, 0], y_send.at[k], y_recv.at[k], across)
+
+    def hand_across(k):
+        if k in SUM_Z:
+            def keep(value):
+                s1[k, 0] = value.astype(BF16)
+            whole_line(k, 1, keep)
+            launch(across_copy(k))
 
     def drain():
         for make, when in pending:
@@ -389,40 +491,38 @@
             else:
                 pl.when(when)(lambda make=make: make().wait_send())
 
-    own2, along2, over2, last2, sent2 = gather_stages(1, xg2)
+    own2, early2, along2, over2, last2, sent2 = gather_stages(1, xg2, NEXT_Y)
 
     def finish(k):
-        for target in range(4):
-            @pl.when(z == target)
-            def _(target=target):
-                value = s2[k, target]
-                if target > 0:
-                    up_copy(k, target)().wait_recv()
-                    value = value + up_in[k, target - 1].astype(F32)
-                if target < 3:
-                    down_copy(k, target)().wait_recv()
-                    value = value + down_in[k, target].astype(F32)
-                s2[k, target] = value
-        residual = (s2[k, z] + hidden_rows(k, 0, cw))
+        def keep(value):
+            s2[0, k, 0] = value
+        whole_line(k, 0, keep)
+        mixed = s2[0, k, 0]
+        if k in SUM_Z:
+            across_copy(k)().wait_recv()
+            mixed = mixed + rb2[k, 0].astype(F32)
+        residual = mixed + hidden_rows(k, 0, cw)
         res_out[:, pl.ds(k * cw, cw)] = residual[:8].astype(BF16)
         res_out[:, pl.ds(half + k * cw, cw)] = residual[8:].astype(BF16)
         xg2[k, me] = residual.astype(BF16)
-        own2(k)
 
     def add_next(scaled, at):
         acc_next[...] += jnp.dot(scaled, wn[at, :], preferred_element_type=F32)
 
+    next_used = [k for name, k in ORDER_NEXT if name == "last"][0]
+
     def project_next(k):
-        if k == 0:
+        if k == next_used:
             weights[4].wait()
-        if k == CHUNKS - 1:
+        if k == ORDER_NEXT[-1][1]:
             drain()
         last2(k)
         consume(xg2, gain_out, add_next, k)
 
-    run([(0, multiply), (1, sum_cores), (2, sum_across), (2, hop(0)), (3, hop(1)), (4, hop(2)),
-         (5, finish), (6, along2(1)), (6, over2(0)), (7, along2(2)), (7, over2(1)), (8, along2(3)),
-         (8, over2(2)), (9, over2(3)), (10, project_next)])
+    run(dict(mult=multiply, sumc=sum_cores, suma=sum_across, hop0=hop(0), hop1=hop(1), hop2=hop(2),
+             yfin=hand_across, fin=finish, own=own2, pre=early2, along1=along2(1), along2=along2(2),
+             along3=along2(3), over0=over2(0), over1=over2(1), over2=over2(2), over3=over2(3),
+             last=project_next), ORDER_NEXT)
 
     next_out[...] = turn(acc_next[...] * inverse_norm()).astype(BF16)
 
@@ -457,11 +557,11 @@
             pltpu.VMEM((CHUNKS, 2, 4, 16, cw), BF16),
             pltpu.VMEM((CHUNKS, 4, 16, cw), BF16),
             pltpu.VMEM((CHUNKS, 4, 16, cw), BF16),
-            pltpu.VMEM((CHUNKS, 4, 16, cw), F32),
-            pltpu.VMEM((CHUNKS, 3, 16, cw), BF16),
-            pltpu.VMEM((CHUNKS, 3, 16, cw), BF16),
-            pltpu.VMEM((CHUNKS, 3, 16, cw), BF16),
-            pltpu.VMEM((CHUNKS, 3, 16, cw), BF16),
+            pltpu.VMEM((2, CHUNKS, 4, 16, cw), F32),
+            pltpu.VMEM((CHUNKS, 2, 3, 16, cw), BF16),
+            pltpu.VMEM((CHUNKS, 2, 3, 16, cw), BF16),
+            pltpu.VMEM((CHUNKS, 2, 3, 16, cw), BF16),
+            pltpu.VMEM((CHUNKS, 2, 3, 16, cw), BF16),
             pltpu.VMEM((KVH, 16, 128), BF16),
             pltpu.VMEM((16, 16, 128), BF16),
             pltpu.VMEM((tokens, 256), F32),
@@ -478,10 +578,10 @@
             dma((CHUNKS,)),
             dma((CHUNKS,)),
             dma((CHUNKS,)),
-            dma((CHUNKS, 3)),
-            dma((CHUNKS, 3)),
-            dma((CHUNKS, 3)),
-            dma((CHUNKS, 3)),
+            dma((CHUNKS, 2, 3)),
+            dma((CHUNKS, 2, 3)),
+            dma((CHUNKS, 2, 3)),
+            dma((CHUNKS, 2, 3)),
         ],
         compiler_params=pltpu.CompilerParams(
             collective_id=0, has_side_effects=True, vmem_limit_bytes=56 * 1024 * 1024

time: 106 us -> 96 us (0.906)
  Pallas kernels: 103 us -> 92 us
    pallas_call x1, Pallas kernels: 103 us -> 92 us  [fused(): pl.pallas_call(block_kernel, out_shape=(jax.ShapeDtypeStruct((share, feat...]
where the time goes in v4:
time: 96 us; the launch traced here: 95.7 us
  Pallas kernels  92 us (96%)
  local copies, waits for them, and re-layouts  3.04 us (3%)
    pallas_call x1, Pallas kernels, fused(): pl.pallas_call(block_kernel, out_shape=(jax.ShapeDtypeStruct((share, feat...  92 us
    unnamed x2, local copies, waits for them, and re-layouts  3.04 us

profile of v4, /device:TPU:0, one launch (start us, length us, event | category | flops | bytes accessed | tf_op | source)
XLA Modules:
  0.0 95.7 jit_solution(15750416583984830763)
XLA Ops:
  0.6 92.0 %attention_block.1 = (bf16[8,16384]{1,0:T(8,128)(2,1)}, bf16[128,128]{1,0:T(8,128)(2,1)}) custom-call(bf16[8,16384]{1,0:T(8,128)(2,1)} %hid.1, s32[1,128]{1,0:T(1,128)} %bitcast.9, f32[1,16384]{1,0:T(1,128)} %bitcast.7, f32[1,16384]{1,0:T(1,128)} %bitcast.8, bf16[16384,128]{1,0:T(8,128)(2,1)} %wq_hbm.1, bf16[64,16384]{1,0:T(8,128)(2,1)} %bitcast.5, ...), custom_call_target="tpu_custom_call" | custom-call | tf_op jit(solution)/shard_map/attention_block/pallas_call | solution.py:541
  92.7 1.7 %copy.13 = bf16[8,16384]{1,0:T(8,128)(2,1)} copy(bf16[8,16384]{1,0:T(8,128)(2,1)} %get-tuple-element.4) | data formatting | bytes 524288
  94.3 1.4 %copy.14 = bf16[128,128]{1,0:T(8,128)(2,1)} copy(bf16[128,128]{1,0:T(8,128)(2,1)} %get-tuple-element.5) | data formatting | bytes 65536

commit v5 on v4

--- a/solution.py
+++ b/solution.py
@@ -9,39 +9,38 @@
 
 KVH = 8
 CHUNKS = 8
-FIRST_Y = (6,)
-NEXT_Y = (7,)
-SUM_Z = (0,)
+FIRST_Y = (7,)
+NEXT_Y = (6, 7)
+SUM_Z = (0, 1)
+OWN, PRE, ALONG1, ALONG2, ALONG3, OVER0, OVER1, OVER2, OVER3, LAST = range(10)
+MULT, SUMC, SUMA, HOP0, HOP1, HOP2, YFIN, FIN = range(10, 18)
 ORDER_FIRST = (
-    ("own", 0), ("own", 2), ("own", 7), ("own", 5), ("own", 1), ("own", 4), ("own", 3), ("own", 6),
-    ("along1", 2), ("along1", 1), ("over0", 2), ("along1", 4), ("along1", 0), ("along1", 3), ("over0", 1),
-    ("along2", 2), ("over0", 4), ("over0", 0), ("pre", 6), ("along2", 1), ("along2", 4), ("along2", 0),
-    ("over1", 2), ("over1", 4), ("over0", 3), ("along2", 3), ("along1", 5), ("along3", 2), ("along3", 4),
-    ("along1", 7), ("over1", 1), ("over1", 0), ("along1", 6), ("over2", 2), ("along3", 1), ("over1", 3),
-    ("over0", 5), ("along3", 3), ("along3", 0), ("along2", 5), ("over2", 4), ("over0", 7), ("along2", 7),
-    ("over3", 2), ("over2", 1), ("last", 2), ("over2", 3), ("over2", 0), ("along2", 6), ("over3", 4),
-    ("over3", 3), ("over1", 5), ("over1", 7), ("along3", 5), ("over3", 0), ("along3", 7), ("last", 3),
-    ("over3", 1), ("last", 0), ("last", 4), ("along3", 6), ("over2", 7), ("over2", 5), ("over3", 5),
-    ("last", 1), ("over3", 7), ("last", 6), ("last", 5), ("last", 7),
+    (OWN, 3), (OWN, 0), (OWN, 6), (OWN, 2), (OWN, 4), (OWN, 1), (ALONG1, 6), (OWN, 7), (OWN, 5),
+    (ALONG1, 2), (ALONG1, 1), (ALONG1, 4), (OVER0, 2), (OVER0, 6), (ALONG2, 6), (PRE, 7), (ALONG1, 3),
+    (OVER0, 4), (ALONG2, 2), (OVER0, 1), (ALONG2, 1), (OVER1, 6), (ALONG3, 6), (ALONG2, 4), (ALONG1, 5),
+    (OVER0, 5), (OVER0, 3), (OVER1, 1), (ALONG1, 0), (OVER1, 2), (ALONG2, 3), (ALONG3, 2), (OVER0, 0),
+    (OVER2, 6), (OVER3, 6), (OVER1, 4), (ALONG1, 7), (ALONG3, 1), (ALONG3, 4), (OVER1, 3), (ALONG2, 0),
+    (OVER2, 1), (OVER2, 2), (ALONG2, 5), (ALONG2, 7), (OVER3, 2), (OVER2, 4), (ALONG3, 3), (OVER3, 1),
+    (OVER3, 4), (OVER1, 5), (OVER1, 0), (ALONG3, 0), (LAST, 1), (ALONG3, 5), (LAST, 2), (OVER2, 3),
+    (LAST, 4), (OVER3, 3), (LAST, 6), (OVER2, 0), (ALONG3, 7), (LAST, 3), (OVER3, 0), (OVER2, 5),
+    (OVER3, 5), (LAST, 7), (LAST, 0), (LAST, 5),
 )
 ORDER_NEXT = (
-    ("mult", 1), ("mult", 0), ("sumc", 1), ("sumc", 0), ("mult", 2), ("hop0", 0), ("sumc", 2), ("mult", 4),
-    ("mult", 7), ("mult", 3), ("sumc", 3), ("suma", 1), ("hop1", 0), ("sumc", 4), ("mult", 5), ("hop0", 1),
-    ("hop2", 0), ("mult", 6), ("hop1", 1), ("suma", 2), ("hop0", 2), ("suma", 3), ("hop0", 3), ("yfin", 0),
-    ("hop1", 2), ("sumc", 5), ("fin", 0), ("hop1", 3), ("suma", 4), ("hop2", 1), ("own", 0), ("sumc", 6),
-    ("sumc", 7), ("hop2", 2), ("hop0", 4), ("fin", 1), ("own", 1), ("hop2", 3), ("suma", 5), ("hop0", 5),
-    ("hop1", 4), ("fin", 2), ("along1", 0), ("own", 2), ("hop2", 4), ("along1", 1), ("suma", 6),
-    ("hop0", 6), ("over0", 0), ("hop1", 5), ("fin", 3), ("along2", 0), ("own", 3), ("suma", 7), ("hop0", 7),
-    ("hop1", 6), ("hop2", 5), ("along1", 2), ("hop2", 6), ("hop1", 7), ("over1", 0), ("over0", 1),
-    ("over0", 2), ("along2", 1), ("over1", 1), ("along3", 0), ("fin", 5), ("own", 5), ("fin", 4),
-    ("own", 4), ("hop2", 7), ("along3", 1), ("fin", 6), ("along2", 2), ("along1", 3), ("own", 6),
-    ("over0", 3), ("fin", 7), ("over2", 1), ("own", 7), ("along1", 4), ("along2", 3), ("over1", 2),
-    ("along1", 5), ("over2", 0), ("along1", 6), ("over1", 3), ("over0", 4), ("along3", 2), ("over0", 5),
-    ("over0", 6), ("pre", 7), ("over3", 1), ("along2", 4), ("along2", 6), ("over3", 0), ("over1", 4),
-    ("along3", 3), ("over2", 3), ("last", 1), ("along2", 5), ("along1", 7), ("over2", 2), ("over1", 6),
-    ("along3", 4), ("last", 0), ("over3", 2), ("over1", 5), ("along3", 6), ("along3", 5), ("along2", 7),
-    ("over2", 4), ("over3", 4), ("over2", 5), ("over3", 3), ("last", 2), ("last", 4), ("over2", 6),
-    ("over3", 5), ("along3", 7), ("over3", 6), ("last", 3), ("last", 5), ("last", 7), ("last", 6),
+    (MULT, 0), (MULT, 4), (MULT, 1), (SUMC, 0), (HOP0, 0), (SUMC, 4), (SUMC, 1), (MULT, 7), (MULT, 5),
+    (MULT, 2), (SUMC, 2), (HOP0, 1), (MULT, 3), (HOP1, 0), (SUMC, 3), (HOP2, 0), (SUMC, 5), (SUMA, 4),
+    (HOP1, 1), (HOP0, 4), (SUMA, 2), (MULT, 6), (HOP0, 2), (YFIN, 0), (HOP1, 4), (SUMC, 6), (HOP2, 1),
+    (HOP1, 2), (SUMA, 3), (HOP0, 3), (SUMA, 5), (FIN, 0), (HOP2, 4), (OWN, 0), (YFIN, 1), (SUMC, 7),
+    (HOP1, 3), (HOP2, 2), (HOP0, 5), (FIN, 4), (SUMA, 6), (HOP0, 6), (ALONG1, 0), (OWN, 4), (HOP1, 5),
+    (FIN, 2), (OWN, 2), (HOP2, 3), (OVER0, 0), (ALONG2, 0), (FIN, 1), (HOP1, 6), (HOP2, 5), (SUMA, 7),
+    (HOP0, 7), (OWN, 1), (FIN, 5), (OVER1, 0), (ALONG1, 4), (FIN, 3), (ALONG3, 0), (ALONG1, 2), (OWN, 3),
+    (OVER2, 0), (HOP2, 6), (HOP1, 7), (OVER3, 0), (OWN, 5), (FIN, 6), (OWN, 6), (ALONG1, 1), (OVER0, 4),
+    (HOP2, 7), (OVER0, 1), (OVER0, 2), (ALONG2, 2), (FIN, 7), (OWN, 7), (ALONG2, 4), (ALONG1, 3),
+    (OVER1, 4), (PRE, 6), (ALONG1, 5), (ALONG2, 1), (LAST, 0), (OVER1, 1), (OVER0, 5), (ALONG3, 4),
+    (OVER1, 2), (PRE, 7), (OVER0, 3), (ALONG2, 3), (OVER2, 4), (ALONG2, 5), (ALONG1, 6), (ALONG3, 1),
+    (ALONG1, 7), (OVER1, 3), (ALONG3, 3), (OVER2, 1), (ALONG3, 2), (OVER1, 5), (OVER2, 2), (ALONG3, 5),
+    (OVER3, 1), (ALONG2, 6), (OVER2, 5), (OVER2, 3), (OVER3, 3), (OVER3, 4), (OVER3, 2), (ALONG2, 7),
+    (LAST, 3), (LAST, 1), (OVER3, 5), (ALONG3, 6), (LAST, 4), (LAST, 2), (LAST, 6), (ALONG3, 7), (LAST, 5),
+    (LAST, 7),
 )
 F32 = jnp.float32
 BF16 = jnp.bfloat16
@@ -293,7 +292,7 @@
         acc[:, :128] += jnp.dot(scaled, wq[at, :], preferred_element_type=F32)
         acc[:, 128:] += lax.dot_general(scaled, wkv[:, at], nt, preferred_element_type=F32)
 
-    first_used = [k for name, k in ORDER_FIRST if name == "last"][0]
+    first_used = [k for name, k in ORDER_FIRST if name == LAST][0]
 
     def project(k):
         if k == first_used:
@@ -302,8 +301,8 @@
         last(k)
         consume(xg1, gain_in, add_projections, k)
 
-    run(dict(own=own, pre=early, along1=along(1), along2=along(2), along3=along(3), over0=over(0),
-             over1=over(1), over2=over(2), over3=over(3), last=project), ORDER_FIRST)
+    run({OWN: own, PRE: early, ALONG1: along(1), ALONG2: along(2), ALONG3: along(3), OVER0: over(0),
+         OVER1: over(1), OVER2: over(2), OVER3: over(3), LAST: project}, ORDER_FIRST)
 
     scale = inverse_norm()
     squares[...] = jnp.zeros_like(squares)
@@ -509,7 +508,7 @@
     def add_next(scaled, at):
         acc_next[...] += jnp.dot(scaled, wn[at, :], preferred_element_type=F32)
 
-    next_used = [k for name, k in ORDER_NEXT if name == "last"][0]
+    next_used = [k for name, k in ORDER_NEXT if name == LAST][0]
 
     def project_next(k):
         if k == next_used:
@@ -519,10 +518,10 @@
         last2(k)
         consume(xg2, gain_out, add_next, k)
 
-    run(dict(mult=multiply, sumc=sum_cores, suma=sum_across, hop0=hop(0), hop1=hop(1), hop2=hop(2),
-             yfin=hand_across, fin=finish, own=own2, pre=early2, along1=along2(1), along2=along2(2),
-             along3=along2(3), over0=over2(0), over1=over2(1), over2=over2(2), over3=over2(3),
-             last=project_next), ORDER_NEXT)
+    run({MULT: multiply, SUMC: sum_cores, SUMA: sum_across, HOP0: hop(0), HOP1: hop(1), HOP2: hop(2),
+         YFIN: hand_across, FIN: finish, OWN: own2, PRE: early2, ALONG1: along2(1), ALONG2: along2(2),
+         ALONG3: along2(3), OVER0: over2(0), OVER1: over2(1), OVER2: over2(2), OVER3: over2(3),
+         LAST: project_next}, ORDER_NEXT)
 
     next_out[...] = turn(acc_next[...] * inverse_norm()).astype(BF16)
 

time: 96 us -> 93.6 us (0.975)
  Pallas kernels: 92 us -> 89.7 us
    pallas_call x1, Pallas kernels: 92 us -> 89.7 us  [fused(): pl.pallas_call(block_kernel, out_shape=(jax.ShapeDtypeStruct((share, feat...]
where the time goes in v5:
time: 93.6 us; the launch traced here: 93.4 us
  Pallas kernels  89.7 us (96%)
  local copies, waits for them, and re-layouts  3.04 us (3%)
    pallas_call x1, Pallas kernels, fused(): pl.pallas_call(block_kernel, out_shape=(jax.ShapeDtypeStruct((share, feat...  89.7 us
    unnamed x2, local copies, waits for them, and re-layouts  3.04 us

profile of v5, /device:TPU:0, one launch (start us, length us, event | category | flops | bytes accessed | tf_op | source)
XLA Modules:
  0.0 93.4 jit_solution(5747150497107059532)
XLA Ops:
  0.6 89.7 %attention_block.1 = (bf16[8,16384]{1,0:T(8,128)(2,1)}, bf16[128,128]{1,0:T(8,128)(2,1)}) custom-call(bf16[8,16384]{1,0:T(8,128)(2,1)} %hid.1, s32[1,128]{1,0:T(1,128)} %bitcast.9, f32[1,16384]{1,0:T(1,128)} %bitcast.7, f32[1,16384]{1,0:T(1,128)} %bitcast.8, bf16[16384,128]{1,0:T(8,128)(2,1)} %wq_hbm.1, bf16[64,16384]{1,0:T(8,128)(2,1)} %bitcast.5, ...), custom_call_target="tpu_custom_call" | custom-call | tf_op jit(solution)/shard_map/attention_block/pallas_call | solution.py:540
  90.4 1.7 %copy.13 = bf16[8,16384]{1,0:T(8,128)(2,1)} copy(bf16[8,16384]{1,0:T(8,128)(2,1)} %get-tuple-element.4) | data formatting | bytes 524288
  92.0 1.4 %copy.14 = bf16[128,128]{1,0:T(8,128)(2,1)} copy(bf16[128,128]{1,0:T(8,128)(2,1)} %get-tuple-element.5) | data formatting | bytes 65536
